TPU v7x, 128 devices: a whole 4x4x4 slice. The times are simulated.
128 devices in a mesh: fsdp: 8 (over x, y_lo), seq: 16 (over y_hi, z, core).
Axes of the slice: x: 4, y: 4 (y_hi: 2, y_lo: 2; y = y_hi * 2 + y_lo), z: 4, core: 2. Of those that a mesh axis runs over, the one named last changes fastest.
Arguments:
- inputs: bfloat16 [20480, 1024], P(('fsdp', 'seq')), may hold values from -6 to 6
- image_ids: int32 [20480], P('fsdp'), may hold values from 0 to 3, as said below
- ln1_gain: bfloat16 [1024], P(('fsdp', 'seq')), may hold values from 0.5 to 1.5
- ln1_shift: bfloat16 [1024], P(('fsdp', 'seq')), may hold values from -1.796875 to 1.796875
- qkv_weight: bfloat16 [1024, 3072], P(('fsdp', 'seq')), may hold values from -0.1875 to 0.1875
- query_bias: bfloat16 [1024], P(('fsdp', 'seq')), may hold values from -1.796875 to 1.796875
- value_bias: bfloat16 [1024], P(('fsdp', 'seq')), may hold values from -0.1796875 to 0.1796875
- out_weight: bfloat16 [1024, 1024], P(('fsdp', 'seq')), may hold values from -6 to 6
- out_bias: bfloat16 [1024], P(('fsdp', 'seq')), may hold values from -1.796875 to 1.796875
- ln2_gain: bfloat16 [1024], P(('fsdp', 'seq')), may hold values from 0.5 to 1.5
- ln2_shift: bfloat16 [1024], P(('fsdp', 'seq')), may hold values from -1.796875 to 1.796875
- fc1_weight: bfloat16 [1024, 4096], P(('fsdp', 'seq')), may hold values from -0.1875 to 0.1875
- fc1_bias: bfloat16 [4096], P(('fsdp', 'seq')), may hold values from -1.796875 to 1.796875
- fc2_weight: bfloat16 [4096, 1024], P(('fsdp', 'seq')), may hold values from -0.09375 to 0.09375
- fc2_bias: bfloat16 [1024], P(('fsdp', 'seq')), may hold values from -1.796875 to 1.796875
- out_grad: bfloat16 [20480, 1024], P(('fsdp', 'seq')), may hold values from -6 to 6
Outputs:
- block_output: bfloat16 [20480, 1024], P(('fsdp', 'seq'))
- input_grad: bfloat16 [20480, 1024], P(('fsdp', 'seq'))
- ln1_gain_grad: float32 [1024], P(('fsdp', 'seq'))
- ln1_shift_grad: float32 [1024], P(('fsdp', 'seq'))
- qkv_weight_grad: float32 [1024, 3072], P(('fsdp', 'seq'))
- query_bias_grad: float32 [1024], P(('fsdp', 'seq'))
- value_bias_grad: float32 [1024], P(('fsdp', 'seq'))
- out_weight_grad: float32 [1024, 1024], P(('fsdp', 'seq'))
- out_bias_grad: float32 [1024], P(('fsdp', 'seq'))
- ln2_gain_grad: float32 [1024], P(('fsdp', 'seq'))
- ln2_shift_grad: float32 [1024], P(('fsdp', 'seq'))
- fc1_weight_grad: float32 [1024, 4096], P(('fsdp', 'seq'))
- fc1_bias_grad: float32 [4096], P(('fsdp', 'seq'))
- fc2_weight_grad: float32 [4096, 1024], P(('fsdp', 'seq'))
- fc2_bias_grad: float32 [1024], P(('fsdp', 'seq'))
Inputs may be any that keep to these rules, and one draw needn't show every extreme that they name: Within each group of 2560 tokens image_ids never falls along the tokens; tokens with one number form one image; in every group one image starts among the group's first 160 tokens and ends among its last 160.
All inputs are finite; a program needn't handle non-finite values.
Results may differ from a plain program's by a relative error of at most 0.01225.
Values may be sent and summed in bfloat16 or wider, within the bound.
No kernel may reach another device: no remote copies, remote signals or barrier semaphores. Data moves between devices by JAX's collectives and lax.ppermute only.
A program may use at most 256 MiB of HBM per device.

v0:
```python
import functools

import jax
import jax.numpy as jnp
from jax import lax
from jax.experimental import pallas as pl
from jax.experimental.pallas import tpu as pltpu
from jax.sharding import Mesh
from jax.sharding import PartitionSpec as P

HEADS = 16
HEAD_DIM = 64
D = 1024
FF = 4096
TOK = 160
GROUP = 2560
HALF = 1280
EPSILON = 1e-06
NEGATIVE = -1e30
TILE = 256
TILES = GROUP // TILE
ALL = ("x", "yl", "yh", "z", "c")
TP = ("z", "c")
XY = ("x", "yl", "yh")
SEQ = ("yh", "z", "c")
BF = jnp.bfloat16
F32 = jnp.float32


def dot(left, right, dims=((1,), (0,))):
    return lax.dot_general(left, right, (dims, ((), ())), preferred_element_type=F32)


def params(mebibytes):
    return pltpu.CompilerParams(vmem_limit_bytes=mebibytes * 1024 * 1024)


def cost(micros):
    return pl.CostEstimate(flops=int(micros * 1e9), bytes_accessed=1 << 20, transcendentals=0)


def whole(*shape):
    return pl.BlockSpec(shape, lambda *_: (0,) * len(shape))


def along(value, axis, by):
    size = 4 if axis in ("x", "z") else 2
    return lax.ppermute(value, axis, [(i, (i + by) % size) for i in range(size)])


def along_y(value, by):
    pairs = []
    for yl in range(2):
        for yh in range(2):
            to = (yh * 2 + yl + by) % 4
            pairs.append((yl * 2 + yh, (to % 2) * 2 + to // 2))
    return lax.ppermute(value, ("yl", "yh"), pairs)


def from_up(value, k):
    return along(value, "z", 4 - k)


def after(value, *done):
    return lax.optimization_barrier((value, *done))[0]


def exchange(value, axes):
    return lax.all_to_all(value, axes, split_axis=0, concat_axis=0, tiled=True)


def project_rows(raw, sv, wh, bias):
    rows = raw.astype(F32)
    center = rows - jnp.mean(rows, -1, keepdims=True)
    spread = jnp.mean(center * center, -1, keepdims=True)
    gain = sv[0:1, :].astype(F32)
    shift = sv[1:2, :].astype(F32)
    normed = (center * lax.rsqrt(spread + EPSILON) * gain + shift).astype(BF)
    mixed = dot(normed, wh[...])
    queries = (mixed[:, 0:64] + bias[0:1, :]).astype(BF) * jnp.asarray(0.125, BF)
    keys = mixed[:, 64:128].astype(BF)
    values = (mixed[:, 128:192] + bias[8:9, :]).astype(BF)
    return normed, jnp.concatenate([queries, jnp.zeros_like(queries)], 1), jnp.concatenate([keys, values], 1)


def choose_head(at, w, sv, heads, wh, bias):
    @pl.when(pl.program_id(0) == 0)
    def _():
        for j in range(16):
            for part in range(2):
                lane = part * 512
                rows = jnp.where(at[0] == 0, w[j, :, lane : lane + 192], w[j, :, lane + 192 : lane + 384])
                wh[j * 64 + part * 32 : j * 64 + part * 32 + 32, :] = rows
                heads[j * 64 + part * 32 : j * 64 + part * 32 + 32, :] = w[j, :, lane : lane + 384]
        for row, place in ((2, 0), (3, 8)):
            value = sv[row : row + 1, 0:64]
            for h in range(1, HEADS):
                value = jnp.where(at[3] == h, sv[row : row + 1, h * 64 : h * 64 + 64], value)
            bias[place : place + 1, :] = value.astype(F32)


def image_range(at, ids):
    first = jnp.zeros_like(ids)
    length = jnp.zeros_like(ids)
    for m in range(4):
        first = jnp.where(ids == m, at[4 + m], first)
        length = jnp.where(ids == m, at[5 + m] - at[4 + m], length)
    return first, length


def masked(values, base, first, length, fill):
    place = lax.broadcasted_iota(jnp.int32, values.shape, 0) - (first - base)
    return jnp.where(jnp.logical_and(place >= 0, place < length), values, fill)


def attend_tile(at, queries, kv, vt, ids, att, o_out, lse_out):
    first, length = image_range(at, ids[0])
    scores = []
    for key_half, keys in enumerate(kv):
        raw = dot(keys[...], queries, ((1,), (1,)))
        base = ((key_half + at[0]) % 2) * HALF
        scores.append(masked(raw, base, first, length, NEGATIVE))
    top = jnp.maximum(jnp.max(scores[0], 0, keepdims=True), jnp.max(scores[1], 0, keepdims=True))
    total = 0.0
    out = 0.0
    for part, values in zip(scores, vt, strict=True):
        part = jnp.exp(part - top)
        total = total + jnp.sum(part, 0, keepdims=True)
        out = out + dot(values[64:128, :], part.astype(BF))
    out = out / total
    o_out[...] = out
    att[...] = out.T.astype(BF)
    lse_out[0] = top + jnp.log(total)


def project_kernel(at, x_a, x_b, w, sv, ids, n1_a, n1_b, q_a, kv_a, q_b, kv_b, heads, att, o_out, lse_out, wh, bias, vt_a, vt_b):
    step = pl.program_id(0)
    choose_head(at, w, sv, heads, wh, bias)

    @pl.when(step < 4)
    def _():
        raw = jnp.where(step < 2, x_a[...], x_b[...]).reshape(4 * TOK, D)
        normed, queries, pairs = project_rows(raw, sv, wh, bias)
        rows = pl.ds(pl.multiple_of((step % 2) * 4 * TOK, 4 * TOK), 4 * TOK)

        def put(n1, q_out, kv_out):
            n1[...] = normed.reshape(2, 2, TOK, D)
            q_out[rows, :] = queries
            kv_out[rows, :] = pairs

        pl.when(step < 2)(lambda: put(n1_a, q_a, kv_a))
        pl.when(step >= 2)(lambda: put(n1_b, q_b, kv_b))

    @pl.when(step == 4)
    def _():
        vt_a[...] = kv_a[...].T
        vt_b[...] = kv_b[...].T

    @pl.when(step >= 4)
    def _():
        tile = step - 4
        queries = q_b[pl.ds(pl.multiple_of(tile * TILE, TILE), TILE), :]
        attend_tile(at, queries, (kv_a, kv_b), (vt_a, vt_b), ids, att, o_out, lse_out)


def project(at, near, far, rows, sv, ids):
    tiles = HALF // TILE
    one = lambda i, at: (jnp.minimum(i, 1), 0, 0, 0)
    two = lambda i, at: (jnp.clip(i - 2, 0, 1), 0, 0, 0)
    late = lambda i: jnp.maximum(i - 4, 0)
    block = lambda index: pl.BlockSpec((2, 2, TOK, D), index)
    tokens = jax.ShapeDtypeStruct((4, 2, TOK, D), BF)
    pairs = jax.ShapeDtypeStruct((HALF, 128), BF)
    return pl.pallas_call(
        project_kernel,
        out_shape=[tokens] * 2
        + [pairs] * 4
        + [
            jax.ShapeDtypeStruct((D, 384), BF),
            jax.ShapeDtypeStruct((HALF, HEAD_DIM), BF),
            jax.ShapeDtypeStruct((HEAD_DIM, HALF), F32),
            jax.ShapeDtypeStruct((tiles, 1, TILE), F32),
        ],
        grid_spec=pltpu.PrefetchScalarGridSpec(
            num_scalar_prefetch=1,
            grid=(4 + tiles,),
            in_specs=[
                block(one),
                block(two),
                whole(16, 32, D),
                whole(8, D),
                pl.BlockSpec((1, 1, TILE), lambda i, at: (1 - at[0], 0, late(i))),
            ],
            out_specs=[block(one), block(two)]
            + [whole(HALF, 128)] * 4
            + [
                whole(D, 384),
                pl.BlockSpec((TILE, HEAD_DIM), lambda i, at: (late(i), 0)),
                pl.BlockSpec((HEAD_DIM, TILE), lambda i, at: (0, late(i))),
                pl.BlockSpec((1, 1, TILE), lambda i, at: (late(i), 0, 0)),
            ],
            scratch_shapes=[pltpu.VMEM((D, 192), BF), pltpu.VMEM((16, HEAD_DIM), F32)] + [pltpu.VMEM((128, HALF), BF)] * 2,
        ),
        compiler_params=params(60),
        cost_estimate=cost(1),
        name="project_attend",
    )(at, near, far, rows, sv, ids)


def attend_kernel(at, q, kv_a, kv_b, ids, att, o_out, lse_out, vt_a, vt_b):
    @pl.when(pl.program_id(0) == 0)
    def _():
        vt_a[...] = kv_a[...].T
        vt_b[...] = kv_b[...].T

    attend_tile(at, q[...], (kv_a, kv_b), (vt_a, vt_b), ids, att, o_out, lse_out)


def attend(at, half, q, kv, ids):
    tiles = HALF // TILE
    pairs = whole(HALF, 128)
    return pl.pallas_call(
        attend_kernel,
        out_shape=(
            jax.ShapeDtypeStruct((HALF, HEAD_DIM), BF),
            jax.ShapeDtypeStruct((HEAD_DIM, HALF), F32),
            jax.ShapeDtypeStruct((tiles, 1, TILE), F32),
        ),
        grid_spec=pltpu.PrefetchScalarGridSpec(
            num_scalar_prefetch=1,
            grid=(tiles,),
            in_specs=[
                pl.BlockSpec((TILE, 128), lambda i, at: (i, 0)),
                pairs,
                pairs,
                pl.BlockSpec((1, 1, TILE), lambda i, at: ((at[0] + half) % 2, 0, i)),
            ],
            out_specs=[
                pl.BlockSpec((TILE, HEAD_DIM), lambda i, at: (i, 0)),
                pl.BlockSpec((HEAD_DIM, TILE), lambda i, at: (0, i)),
                pl.BlockSpec((1, 1, TILE), lambda i, at: (i, 0, 0)),
            ],
            scratch_shapes=[pltpu.VMEM((128, HALF), BF)] * 2,
        ),
        compiler_params=params(60),
        cost_estimate=cost(1),
        name="attend",
    )(at, q, *kv, ids)


def attend_back_kernel(at, q_a, q_b, kv_a, kv_b, do_in, o_a, o_b, lse_a, lse_b, ids, g_abs, g_a, g_b, q, kv, do, kt, dq, dkv):
    tile = pl.program_id(0)
    yh = at[0]

    @pl.when(tile == 0)
    def _():
        for ref, one, two in ((q, q_a, q_b), (kv, kv_a, kv_b)):
            ref[0:HALF, :] = one[...]
            ref[HALF:GROUP, :] = two[...]
        kt[...] = kv[...].T
        for half in range(2):
            start = ((half + yh) % 2) * HALF
            for s in range(8):
                packed = do_in[half * 8 + s]
                block = jnp.concatenate([packed[:, 0:64], packed[:, 64:128]], 0)
                block = jnp.concatenate([jnp.zeros_like(block), block], 1)
                do[pl.ds(pl.multiple_of(start + s * TOK, TOK), TOK), :] = block
        dkv[...] = jnp.zeros_like(dkv)

    near = tile < TILES // 2

    first, length = image_range(at, ids[0])
    o_tile = jnp.where(near, o_a[...], o_b[...])
    lse = jnp.where(near, lse_a[0], lse_b[0])
    rows = pl.ds(pl.multiple_of(tile * TILE, TILE), TILE)
    queries = q[rows, :]
    grads = do[rows, :]
    delta = jnp.sum(o_tile * grads[:, 64:128].astype(F32).T, 0, keepdims=True)
    dq_tile = 0.0
    for half in range(2):
        here = slice(half * HALF, half * HALF + HALF)
        scores = dot(kv[here, :], queries, ((1,), (1,)))
        base = ((half + yh) % 2) * HALF
        probs = jnp.exp(masked(scores, base, first, length, NEGATIVE) - lse)
        probs_grad = dot(kv[here, :], grads, ((1,), (1,)))
        scores_grad = (probs * (probs_grad - delta)).astype(BF)
        dkv[here, :] += dot(scores_grad, queries) + dot(probs.astype(BF), grads)
        dq_tile = dq_tile + dot(kt[0:64, here], scores_grad)
    dq[rows, :] = (dq_tile.T * 0.125).astype(BF)

    @pl.when(tile == TILES - 1)
    def _():
        for ref, half in ((g_a, 0), (g_b, 1)):
            here = slice(half * HALF, half * HALF + HALF)
            ref[:, 0:64] = dq[here, :]
            ref[:, 64:192] = dkv[here, :].astype(BF)
            for s in range(8):
                block = ref[s * TOK : s * TOK + TOK, :]
                to = ((half + yh) % 2) * 8 + s
                g_abs[to, 0:TOK, :] = block[:, 0:128]
                g_abs[to, TOK : TOK + 80, :] = jnp.concatenate([block[0:80, 128:192], block[80:TOK, 128:192]], 1)


def attend_back(at, q, kv, do, o, lse, ids):
    pairs = whole(HALF, 128)
    last = TILES // 2 - 1
    one = lambda i: jnp.minimum(i, last)
    two = lambda i: jnp.maximum(i - last - 1, 0)
    wide = pltpu.VMEM((GROUP, 128), BF)
    return pl.pallas_call(
        attend_back_kernel,
        out_shape=(
            jax.ShapeDtypeStruct((HEADS, 240, 128), BF),
            jax.ShapeDtypeStruct((HALF, 192), BF),
            jax.ShapeDtypeStruct((HALF, 192), BF),
        ),
        grid_spec=pltpu.PrefetchScalarGridSpec(
            num_scalar_prefetch=1,
            grid=(TILES,),
            in_specs=[pairs] * 4
            + [whole(HEADS, TOK // 2, 128)]
            + [pl.BlockSpec((HEAD_DIM, TILE), lambda i, at, f=f: (0, f(i))) for f in (one, two)]
            + [pl.BlockSpec((1, 1, TILE), lambda i, at, f=f: (f(i), 0, 0)) for f in (one, two)]
            + [pl.BlockSpec((1, 1, TILE), lambda i, at: ((at[0] + i // (last + 1)) % 2, 0, i % (last + 1)))],
            out_specs=[whole(HEADS, 240, 128), whole(HALF, 192), whole(HALF, 192)],
            scratch_shapes=[
                wide,
                wide,
                wide,
                pltpu.VMEM((128, GROUP), BF),
                pltpu.VMEM((GROUP, HEAD_DIM), BF),
                pltpu.VMEM((GROUP, 128), F32),
            ],
        ),
        compiler_params=params(60),
        cost_estimate=cost(20),
        name="attend_back",
    )(at, *q, *kv, do, *o, *lse, ids)


def feed_kernel(at, *refs):
    blocks, refs = refs[:8], refs[8:]
    x, w_out, sv, rows, bias, dy, resid_out, att_out, y_out, dn2_other, dn2_own, w1_out, w2_out, b1_out = refs[:14]
    wide, w1, w2, b1, w1_grad, w2_grad = refs[14:]
    step = pl.program_id(0)
    z, core = at[1], at[2]
    own = step >= 1

    @pl.when(step == 0)
    def _():
        for j in range(16):
            w1[j * 64 : j * 64 + 32, :] = rows[j, 0:32, 0:512]
            w1[j * 64 + 32 : j * 64 + 64, :] = rows[j, 0:32, 512:1024]
            w2[j * 32 : j * 32 + 32, :] = rows[j, 32:64, :]
            b1[0:1, j * 32 : j * 32 + 32] = bias[j, 0:1, 0:32].astype(F32)
        b1_out[...] = jnp.zeros_like(b1_out)
        w1_grad[...] = jnp.zeros_like(w1_grad)
        w2_grad[...] = jnp.zeros_like(w2_grad)

    for k in range(4):
        mine, theirs = (block[:, 0].reshape(4 * TOK, 128) for block in (blocks[k], blocks[4 + k]))
        one = jnp.where(core == 0, mine, theirs)
        two = jnp.where(core == 0, theirs, mine)
        for h in range(2):
            lane = pl.multiple_of(h * 512 + ((z + k) % 4) * 128, 128)
            here = slice(h * 64, h * 64 + 64)
            wide[:, pl.ds(lane, 128)] = jnp.concatenate([one[:, here], two[:, here]], 1)
    resid = x[:, 0].reshape(4 * TOK, D).astype(F32) + dot(wide[...], w_out[...]) + sv[4:5, :].astype(F32)

    for k in range(4):

        @pl.when(jnp.logical_and(own, z == k))
        def _(k=k):
            resid_out[...] = resid[k * TOK : k * TOK + TOK]
            att_out[...] = wide[k * TOK : k * TOK + TOK, :]

    center = resid - jnp.mean(resid, -1, keepdims=True)
    spread = jnp.mean(center * center, -1, keepdims=True)
    normed = (center * lax.rsqrt(spread + EPSILON) * sv[5:6, :].astype(F32) + sv[6:7, :].astype(F32)).astype(BF)
    pre = dot(normed, w1[...]) + b1[0:1, :]
    cdf = 0.5 * (1.0 + lax.erf(pre * (0.5**0.5)))
    hidden = (pre * cdf).astype(BF)
    slope = cdf + pre * jnp.exp(-0.5 * pre * pre) * 0.3989422804014327
    dy_rows = dy[:, 0].reshape(4 * TOK, D)
    hidden_grad = dot(dy_rows, w2[...], ((1,), (1,)))
    pre_grad = (hidden_grad * slope).astype(BF)
    normed_grad = dot(pre_grad, w1[...], ((1,), (1,))).astype(BF).reshape(4, TOK, D)
    y_out[:, 0] = dot(hidden, w2[...]).astype(BF).reshape(4, TOK, D)
    w2_grad[...] += dot(hidden, dy_rows, ((0,), (0,)))
    w1_grad[...] += dot(normed, pre_grad, ((0,), (0,)))
    b1_out[...] += jnp.sum(pre_grad.astype(F32), 0, keepdims=True)

    @pl.when(own)
    def _():
        dn2_own[...] = normed_grad

    @pl.when(jnp.logical_not(own))
    def _():
        dn2_other[...] = normed_grad

    @pl.when(step == 1)
    def _():
        w1_out[...] = w1_grad[...].astype(BF).reshape(16, 64, 512)
        w2_out[...] = w2_grad[...].astype(BF).reshape(16, 32, D)


def feed(at, att_own, att_other, x, w_out, sv, rows, dy):
    core_of = lambda i, at: jnp.where(i >= 1, at[2], 1 - at[2])
    tok_spec = lambda width: pl.BlockSpec((4, 1, TOK, width), lambda i, at: (0, core_of(i, at), 0, 0))
    return pl.pallas_call(
        feed_kernel,
        out_shape=(
            jax.ShapeDtypeStruct((TOK, D), F32),
            jax.ShapeDtypeStruct((TOK, D), BF),
            jax.ShapeDtypeStruct((4, 2, TOK, D), BF),
            jax.ShapeDtypeStruct((4, TOK, D), BF),
            jax.ShapeDtypeStruct((4, TOK, D), BF),
            jax.ShapeDtypeStruct((16, 64, 512), BF),
            jax.ShapeDtypeStruct((16, 32, D), BF),
            jax.ShapeDtypeStruct((1, 512), F32),
        ),
        grid_spec=pltpu.PrefetchScalarGridSpec(
            num_scalar_prefetch=1,
            grid=(2,),
            in_specs=[tok_spec(128)] * 8
            + [
                tok_spec(D),
                whole(D, D),
                whole(8, D),
                whole(16, 64, D),
                pl.BlockSpec((16, 8, D), lambda i, at: (0, 8, 0)),
                tok_spec(D),
            ],
            out_specs=[
                whole(TOK, D),
                whole(TOK, D),
                tok_spec(D),
                whole(4, TOK, D),
                whole(4, TOK, D),
                whole(16, 64, 512),
                whole(16, 32, D),
                whole(1, 512),
            ],
            scratch_shapes=[
                pltpu.VMEM((4 * TOK, D), BF),
                pltpu.VMEM((D, 512), BF),
                pltpu.VMEM((512, D), BF),
                pltpu.VMEM((8, 512), F32),
                pltpu.VMEM((D, 512), F32),
                pltpu.VMEM((512, D), F32),
            ],
        ),
        compiler_params=params(56),
        cost_estimate=cost(20),
        name="out_feed",
    )(at, *att_own, *att_other, x, w_out, sv, rows, rows, dy)


def mix_kernel(at, own, came, *outs):
    for k in range(4):
        here = pl.ds((at[1] + k) % 4, 1)
        outs[k][...] = (own[here][0].astype(F32) + came[here][0].astype(F32)).astype(BF)


def mix(at, own, came):
    return pl.pallas_call(
        mix_kernel,
        out_shape=[jax.ShapeDtypeStruct((TOK, D), BF)] * 4,
        grid_spec=pltpu.PrefetchScalarGridSpec(
            num_scalar_prefetch=1,
            grid=(1,),
            in_specs=[whole(4, TOK, D)] * 2,
            out_specs=[whole(TOK, D)] * 4,
        ),
        compiler_params=params(60),
        cost_estimate=cost(2),
        name="mix",
    )(at, own, came)


def norm_back(values, gain, grad):
    center = values - jnp.mean(values, -1, keepdims=True)
    spread = jnp.mean(center * center, -1, keepdims=True)
    r = lax.rsqrt(spread + EPSILON)
    n = center * r
    e = grad * gain
    inner = r * (e - jnp.mean(e, -1, keepdims=True) - n * jnp.mean(e * n, -1, keepdims=True))
    return inner, jnp.sum(grad * n, 0, keepdims=True), jnp.sum(grad, 0, keepdims=True)


def middle_kernel(m0, m1, m2, m3, resid, dy, sv, w_out, resid_grad_out, branch_out, att_grad_out, sums):
    grad = m0[...].astype(F32) + m1[...].astype(F32) + m2[...].astype(F32) + m3[...].astype(F32)
    dy_f = dy[...].astype(F32)
    part, gain_grad, shift_grad = norm_back(resid[...], sv[5:6, :].astype(F32), grad)
    resid_grad = dy_f + part
    resid_grad_out[...] = resid_grad
    branch = resid_grad.astype(BF)
    branch_out[...] = branch
    sums[0:1, :] = jnp.sum(branch.astype(F32), 0, keepdims=True)
    sums[1:2, :] = gain_grad
    sums[2:3, :] = shift_grad
    sums[3:4, :] = jnp.sum(dy_f, 0, keepdims=True)
    att_grad = dot(branch, w_out[...], ((1,), (1,))).astype(BF)
    for h in range(HEADS):
        lane = h * 64
        att_grad_out[h] = jnp.concatenate(
            [att_grad[0:80, lane : lane + 64], att_grad[80:160, lane : lane + 64]], 1
        )


def middle(parts, resid, dy, sv, w_out):
    return pl.pallas_call(
        middle_kernel,
        out_shape=(
            jax.ShapeDtypeStruct((TOK, D), F32),
            jax.ShapeDtypeStruct((TOK, D), BF),
            jax.ShapeDtypeStruct((HEADS, TOK // 2, 128), BF),
            jax.ShapeDtypeStruct((4, D), F32),
        ),
        grid=(1,),
        in_specs=[whole(TOK, D)] * 6 + [whole(8, D), whole(D, D)],
        out_specs=[whole(TOK, D), whole(TOK, D), whole(HEADS, TOK // 2, 128), whole(4, D)],
        compiler_params=params(16),
        cost_estimate=cost(5),
        name="middle",
    )(*parts, resid, dy, sv, w_out)


def last_kernel(g_a, g_b, w, x, resid_grad, sv, out, sums, biases, total):
    step = pl.program_id(0)

    @pl.when(step == 0)
    def _():
        total[...] = jnp.zeros_like(total)

    for k in range(2):
        pair = []
        for packed in (g_a[k], g_b[k]):
            values = jnp.concatenate([packed[160:240, 0:64], packed[160:240, 64:128]], 0)
            pair += [packed[0:160, :], values]
        pair = jnp.concatenate(pair, 1)
        total[...] += dot(pair, w[k], ((1,), (1,)))
        biases[k] = jnp.sum(pair.astype(F32), 0, keepdims=True)

    @pl.when(step == 3)
    def _():
        part, gain_grad, shift_grad = norm_back(x[...].astype(F32), sv[0:1, :].astype(F32), total[...])
        out[...] = (resid_grad[...] + part).astype(BF)
        sums[0:1, :] = gain_grad
        sums[1:2, :] = shift_grad


def last(g, w, x, resid_grad, sv):
    return pl.pallas_call(
        last_kernel,
        out_shape=(
            jax.ShapeDtypeStruct((TOK, D), BF),
            jax.ShapeDtypeStruct((2, D), F32),
            jax.ShapeDtypeStruct((8, 1, 384), F32),
        ),
        grid=(4,),
        in_specs=[
            pl.BlockSpec((2, 240, 128), lambda i: (i, 0, 0)),
            pl.BlockSpec((2, 240, 128), lambda i: (i + 4, 0, 0)),
            pl.BlockSpec((2, D, 384), lambda i: (i, 0, 0)),
            whole(TOK, D),
            whole(TOK, D),
            whole(8, D),
        ],
        out_specs=[whole(TOK, D), whole(2, D), pl.BlockSpec((2, 1, 384), lambda i: (i, 0, 0))],
        scratch_shapes=[pltpu.VMEM((TOK, D), F32)],
        compiler_params=params(48),
        cost_estimate=cost(15),
        name="last",
    )(g, g, w, x, resid_grad, sv)


def body(
    inputs,
    image_ids,
    ln1_gain,
    ln1_shift,
    qkv_weight,
    query_bias,
    value_bias,
    out_weight,
    out_bias,
    ln2_gain,
    ln2_shift,
    fc1_weight,
    fc1_bias,
    fc2_weight,
    fc2_bias,
    out_grad,
):
    xi, yl, yh, zi, ci = (lax.axis_index(name) for name in ALL)
    zc = zi * 2 + ci
    where_at = jnp.arange(16)
    starts = jnp.sum((image_ids[:, None] < where_at[None, :] - 4).astype(jnp.int32), 0)
    at = jnp.where(where_at == 0, yh, jnp.where(where_at == 1, zi, jnp.where(where_at == 2, ci, yh * 8 + zc)))
    at = jnp.where(where_at < 4, at, starts).astype(jnp.int32)

    near = lax.all_gather(inputs, TP, axis=0, tiled=True).reshape(4, 2, TOK, D)
    crossed = along(inputs, "yh", 1)

    qkv = qkv_weight.reshape(8, 3, 2, 8, HEAD_DIM).transpose(3, 0, 2, 1, 4).reshape(8, 8, 384)
    small = jnp.stack(
        [ln1_gain, ln1_shift, query_bias, value_bias, out_bias, ln2_gain, ln2_shift, fc2_bias], 1
    )
    small = jnp.broadcast_to(jnp.pad(small, ((0, 0), (0, 120)))[None], (8, 8, 128))
    fc1 = fc1_weight.reshape(8, 16, 8, 32).transpose(2, 0, 1, 3).reshape(8, 8, 512)
    columns = exchange(jnp.concatenate([qkv, small, fc1], 2), TP)
    far = lax.all_gather(after(crossed, columns), TP, axis=0, tiled=True).reshape(4, 2, TOK, D)
    columns = columns.reshape(64, D)

    fc1 = jnp.concatenate([columns[0:32, 512:], columns[32:64, 512:]], 1)
    columns = jnp.concatenate([columns[0:32, 0:512], columns[32:64, 0:512]], 1)
    spread = lambda v: exchange(jnp.broadcast_to(v[None], (16, *v.shape)), XY)
    first = spread(jnp.concatenate([columns, out_weight], 0))
    bias = jnp.pad(fc1_bias[None], ((0, 7), (0, D - 32)))
    rows = spread(after(jnp.concatenate([fc1, fc2_weight, bias], 0), first))
    sv = jnp.concatenate([first[:, 0:32, 384:392], first[:, 0:32, 896:904]], 1).reshape(D, 8).T
    sent = jnp.concatenate([out_grad, first[:, 32:40].reshape(128, D)], 0)
    sent = lax.all_gather(sent, TP, axis=0, tiled=False)
    w_out = sent[:, TOK:].reshape(8, 16, 8, D).transpose(1, 0, 2, 3).reshape(D, D)
    dy_all = sent.reshape(4, 2, TOK + 128, D)

    ids = image_ids.reshape(2, 1, HALF)
    n1_near, n1_far, q_near, kv_near, q_far, kv_far, heads, att_far, o_far, lse_far = project(
        at, near, far, first, sv, ids
    )
    q, kv = (q_near, q_far), (kv_near, kv_far)
    theirs = along(att_far, "yh", 1)
    att_near, o_near, lse_near = attend(at, 0, after(q[0], att_far), kv, ids)
    att_two = jnp.where(
        yh == 0, jnp.concatenate([att_near, theirs], 1), jnp.concatenate([theirs, att_near], 1)
    )
    att_two = after(att_two, rows)
    att_own = [att_two] + [from_up(att_two, k) for k in (1, 2, 3)]
    att_other = [along(after(block, w_out), "c", 1) for block in att_own]
    w_qkv = lax.all_gather(after(heads, *att_other), TP, axis=0, tiled=False)
    split = lambda blocks: [block.reshape(4, 2, TOK, 128) for block in blocks]
    resid, att_tok, y_part, dn2_other, dn2_own, fc1_grad, fc2_grad, b1_grad = feed(
        at, split(att_own), split(att_other), near, w_out, sv, rows, dy_all
    )

    mixed = mix(at, dn2_own, along(dn2_other, "c", 1))
    parts = [mixed[0]] + [along(mixed[k], "z", k) for k in (1, 2, 3)]
    fc2_grad = exchange(fc2_grad, XY)
    parts = [after(parts[0], fc2_grad)] + parts[1:]
    resid_grad, branch_grad, att_grad, mid_sums = middle(parts, resid, out_grad, sv, w_out)
    do = exchange(after(att_grad, w_qkv), SEQ)
    turn = ((0,), (0,))

    g, g_near, g_far = attend_back(
        at, q, kv, do, (o_near, o_far), (lse_near, lse_far), ids
    )

    out_w = dot(att_tok, branch_grad, turn).astype(BF)
    out_w = lax.psum_scatter(after(out_w, do), TP, scatter_dimension=0, tiled=True)

    fc1_grad = exchange(after(fc1_grad, do), XY)
    g_tok = exchange(after(g, fc1_grad), SEQ)
    fc1_grad = jnp.sum(fc1_grad.astype(F32), 0).reshape(8, 8, 512)
    fc1_grad = exchange(after(fc1_grad, g_tok), TP)
    fc1_grad = fc1_grad.reshape(8, 8, 16, 32).transpose(1, 2, 0, 3).reshape(8, FF)

    summed = lax.psum_scatter(after(y_part, *parts).reshape(HALF, D), TP, scatter_dimension=0, tiled=True)
    outputs = resid + summed.astype(F32) + sv[7].astype(F32)

    qkv_grad = dot(n1_near.reshape(HALF, D), g_near, turn) + dot(n1_far.reshape(HALF, D), g_far, turn)
    qkv_grad = qkv_grad.astype(BF)
    pick = lambda v, axis, place: lax.dynamic_index_in_dim(v, place, axis, keepdims=False)
    out_w = after(out_w, qkv_grad).reshape(4, 2, 2, 8, D)
    total = pick(out_w, 0, xi).astype(F32)
    for k in (1, 2, 3):
        total = total + along(pick(out_w, 0, (xi + k) % 4), "x", k).astype(F32)
    out_w = total.astype(BF)
    g_tok = after(g_tok, out_w)
    input_grad, norm_sums, biases = last(g_tok, w_qkv, inputs, resid_grad, sv)
    fc2_grad = jnp.sum(after(fc2_grad, norm_sums).astype(F32), 0)
    biases = biases.reshape(8, 2, 3, HEAD_DIM).transpose(2, 1, 0, 3).reshape(3, D)
    vectors = jnp.concatenate([norm_sums, biases[0:1], biases[2:3], mid_sums])
    vectors = vectors.reshape(8, 128, 8).transpose(1, 0, 2)
    mine = jnp.arange(8)[None, :, None] == zc
    b1_part = jnp.where(mine, b1_grad.reshape(16, 1, 32), 0.0).reshape(128, 4, 8)
    b1_part = jnp.pad(b1_part, ((0, 0), (0, 4), (0, 0)))
    vectors = jnp.concatenate([vectors, b1_part], 2)
    high = vectors.astype(BF)
    low = (vectors - high.astype(F32)).astype(BF)

    final = jnp.concatenate([qkv_grad.reshape(128, 8, 192), high, low], 2)
    final = after(final, out_w)
    out_w = after(out_w, norm_sums)
    by_y = lambda y: pick(pick(out_w, 0, y % 2), 0, y // 2)
    yi = yh * 2 + yl
    total = by_y(yi).astype(F32)
    for k in (1, 2, 3):
        total = total + along_y(by_y((yi + k) % 4), k).astype(F32)
    out_w = lax.ppermute(total, ALL, [(j * 8 + s, (2 * s + j // 8) * 8 + j % 8) for j in range(16) for s in range(8)])
    final = exchange(final, ALL).astype(F32)
    qkv_grad = jnp.sum(final[:, :, 0:192].reshape(8, HEADS, 8, 192), 0)
    qkv_grad = qkv_grad.reshape(HEADS, 8, 3, HEAD_DIM).transpose(1, 2, 0, 3).reshape(8, 3 * D)
    vectors = jnp.sum(final[:, :, 192:208] + final[:, :, 208:224], 0)
    fc1_bias_grad = vectors[0:4, 8:16].reshape(32)
    vectors = vectors[:, 0:8]
    return (
        outputs.astype(BF),
        input_grad,
        vectors[0],
        vectors[1],
        qkv_grad,
        vectors[2],
        vectors[3],
        out_w,
        vectors[4],
        vectors[5],
        vectors[6],
        fc1_grad,
        fc1_bias_grad,
        fc2_grad,
        vectors[7],
    )


def solution(mesh):
    fine = Mesh(mesh.devices.reshape(4, 2, 2, 4, 2), ALL)
    rows = P(ALL, None)
    vec = P(ALL)
    return jax.shard_map(
        body,
        mesh=fine,
        in_specs=(rows, P(("x", "yl")), vec, vec, rows, vec, vec, rows, vec, vec, vec, rows, vec, rows, vec, rows),
        out_specs=(rows, rows, vec, vec, rows, vec, vec, rows, vec, vec, vec, rows, vec, rows, vec),
        check_vma=False,
    )
```

profile of v0, /device:TPU:0, one launch (start us, length us, event | category | flops | bytes accessed | tf_op | source)
XLA Modules:
  0.0 311.1 jit_solution(5227925053666287677)
XLA Ops:
  8.0 3.4 %collective-permute-start = (bf16[160,1024]{1,0:T(8,128)(2,1)}, bf16[160,1024]{1,0:T(8,128)(2,1)S(1)}, u32[]{:S(2)}, u32[]{:S(2)}) collective-permute-start(bf16[160,1024]{1,0:T(8,128)(2,1)} %x.7), channel_id=1, source_target_pairs={{0,8},{8,0},{1,9},{9,1},{2,10},{10,2},{3,11},{11,3},{4,12},{12,4},... | collective-permute-start | bytes 983048 | tf_op jit(solution)/shard_map/ppermute | solution.py:48
  11.3 1.1 reshape.176
  14.8 11.3 %all_to_all.45 = bf16[8,8,1024]{2,1,0:T(8,128)(2,1)S(1)} all-to-all(bf16[8,8,1024]{2,1,0:T(8,128)(2,1)S(1)} %pad_maximum_fusion.3), channel_id=1, replica_groups=mesh['x'=4,'yl'=2,'yh'=2,'z'=4,'c'=2] {'z','c'}, dimensions={0} | all-to-all | bytes 262144 | tf_op jit(solution)/shard_map/all_to_all | solution.py:69
  27.1 24.7 %all_to_all.46.w = bf16[16,40,1024]{2,1,0:T(8,128)(2,1)S(1)} all-to-all(bf16[16,40,1024]{2,1,0:T(8,128)(2,1)S(1)} %broadcast_in_dim.73), channel_id=1, replica_groups=mesh['x'=4,'yl'=2,'yh'=2,'z'=4,'c'=2] {'x','yl','yh'}, dimensions={0} | all-to-all | bytes 2621440 | tf_op jit(solution)/shard_map/all_to_all | solution.py:69
  52.8 1.7 broadcast_in_dim.75
  54.5 4.6 %all-to-all-start.2 = ((bf16[16,72,1024]{2,1,0:T(8,128)(2,1)}), bf16[16,72,1024]{2,1,0:T(8,128)(2,1)}, u32[]{:S(2)}, u32[]{:S(2)}) async-start(bf16[16,72,1024]{2,1,0:T(8,128)(2,1)} %broadcast_in_dim.75), calls=%async_computation.2 | async-start | bytes 4718592 | tf_op jit(solution)/shard_map/all_to_all | solution.py:69
  61.3 6.3 %all-gather.9.cloned.1.call-done = bf16[1280,1024]{1,0:T(8,128)(2,1)} async-done(((bf16[160,1024]{1,0:T(8,128)(2,1)}), bf16[1280,1024]{1,0:T(8,128)(2,1)}) %all-gather.9.cloned.1.call-update) | async-done | bytes 2621456 | tf_op jit(solution)/shard_map/all_gather | solution.py:613
  67.6 21.2 %project_attend.1 = (bf16[4,2,160,1024]{3,2,1,0:T(8,128)(2,1)}, bf16[4,2,160,1024]{3,2,1,0:T(8,128)(2,1)}, bf16[1280,128]{1,0:T(8,128)(2,1)}, bf16[1280,128]{1,0...) custom-call(s32[16]{0:T(128)} %compare_select_fusion.3.at, ...), custom_call_target="tpu_custom_call" | custom-call | flops 1000000000 | bytes 1048576 | tf_op jit(solution)/shard_map/project_attend/pallas_call | solution.py:174
  88.8 3.1 collective-permute-start.1
  91.9 11.0 %attend.1 = (bf16[1280,64]{1,0:T(8,128)(2,1)}, f32[64,1280]{1,0:T(8,128)}, f32[5,1,256]{2,1,0:T(1,128)}) custom-call(s32[16]{0:T(128)} %compare_select_fusion.3.at, bf16[1280,128]{1,0:T(8,128)(2,1)} %get-tuple-element.74.q.q_a, bf16[1280,128]{1,0:T(8,128)(2,1)} %get-tuple-element.75.kv_a, bf16[1280,128]{1,0:T(8,128)(2,1)} %get-tuple-element.76.kv_b, ...), custom_call_target="tpu_custom_call" | custom-call | flops 1000000000 | bytes 1048576 | tf_op jit(solution)/shard_map/attend/pallas_call | solution.py:222
  102.9 1.5 maximum_select_fusion
  104.4 1.7 collective-permute-start.2
  107.0 1.1 collective-permute-start.4
  108.1 1.8 slice_bitcast_fusion
  109.9 1.6 copy.107
  111.4 3.6 %collective-permute-done.2 = bf16[1280,128]{1,0:T(8,128)(2,1)S(1)} collective-permute-done((bf16[1280,128]{1,0:T(8,128)(2,1)S(1)}, bf16[1280,128]{1,0:T(8,128)(2,1)S(1)}, u32[]{:S(2)}, u32[]{:S(2)}) %collective-permute-start.2) | collective-permute-done | bytes 327712 | tf_op jit(solution)/shard_map/ppermute | solution.py:48
  115.0 3.2 %collective-permute-done.3 = bf16[1280,128]{1,0:T(8,128)(2,1)S(1)} collective-permute-done((bf16[1280,128]{1,0:T(8,128)(2,1)S(1)}, bf16[1280,128]{1,0:T(8,128)(2,1)S(1)}, u32[]{:S(2)}, u32[]{:S(2)}) %collective-permute-start.3) | collective-permute-done | bytes 327712 | tf_op jit(solution)/shard_map/ppermute | solution.py:48
  118.2 5.7 %collective-permute-done.4 = bf16[1280,128]{1,0:T(8,128)(2,1)S(1)} collective-permute-done((bf16[1280,128]{1,0:T(8,128)(2,1)S(1)}, bf16[1280,128]{1,0:T(8,128)(2,1)S(1)}, u32[]{:S(2)}, u32[]{:S(2)}) %collective-permute-start.4) | collective-permute-done | bytes 327712 | tf_op jit(solution)/shard_map/ppermute | solution.py:48
  124.0 1.6 collective-permute-done.8
  126.3 22.9 %out_feed.1 = (f32[160,1024]{1,0:T(8,128)}, bf16[160,1024]{1,0:T(8,128)(2,1)}, bf16[4,2,160,1024]{3,2,1,0:T(8,128)(2,1)}, bf16[4,160,1024]{2,1,0:T(8,128)(2,1)},...) custom-call(s32[16]{0:T(128)} %compare_select_fusion.3.at, ...), custom_call_target="tpu_custom_call" | custom-call | flops 20000000000 | bytes 1048576 | tf_op jit(solution)/shard_map/out_feed/pallas_call | solution.py:410
  149.4 5.0 %all-to-all-start.3 = ((bf16[16,32,1024]{2,1,0:T(8,128)(2,1)}), bf16[16,32,1024]{2,1,0:T(8,128)(2,1)}, u32[]{:S(2)}, u32[]{:S(2)}) async-start(bf16[16,32,1024]{2,1,0:T(8,128)(2,1)} %get-tuple-element.89), calls=%async_computation.3 | async-start | bytes 2097152 | tf_op jit(solution)/shard_map/all_to_all | solution.py:69
  154.4 1.1 copy-done.25
  155.5 3.9 %mix.1 = (bf16[160,1024]{1,0:T(8,128)(2,1)}, bf16[160,1024]{1,0:T(8,128)(2,1)}, bf16[160,1024]{1,0:T(8,128)(2,1)}, bf16[160,1024]{1,0:T(8,128)(2,1)}) custom-call(s32[16]{0:T(128)} %compare_select_fusion.3.at, bf16[4,160,1024]{2,1,0:T(8,128)(2,1)} %get-tuple-element.86.own, bf16[4,160,1024]{2,1,0:T(8,128)(2,1)} %copy-done.25), custom_call_target="tpu_custom_call" | custom-call | flops 2000000000 | bytes 1048576 | tf_op jit(solution)/shard_map/mix/pallas_call | solution.py:466
  159.5 2.4 collective-permute-start.11
  161.9 1.2 collective-permute-start.12
  163.1 10.4 %all-to-all-done.3 = bf16[16,32,1024]{2,1,0:T(8,128)(2,1)} async-done(((bf16[16,32,1024]{2,1,0:T(8,128)(2,1)}), bf16[16,32,1024]{2,1,0:T(8,128)(2,1)}, u32[]{:S(2)}, u32[]{:S(2)}) %all-to-all-start.3) | async-done | bytes 1048608 | tf_op jit(solution)/shard_map/all_to_all | solution.py:69
  173.4 4.2 %collective-permute-done.10.m1 = bf16[160,1024]{1,0:T(8,128)(2,1)S(1)} collective-permute-done((bf16[160,1024]{1,0:T(8,128)(2,1)}, bf16[160,1024]{1,0:T(8,128)(2,1)S(1)}, u32[]{:S(2)}, u32[]{:S(2)}) %collective-permute-start.10) | collective-permute-done | bytes 327712 | tf_op jit(solution)/shard_map/ppermute | solution.py:48
  180.4 3.3 %middle.1 = (f32[160,1024]{1,0:T(8,128)S(1)}, bf16[160,1024]{1,0:T(8,128)(2,1)S(1)}, bf16[16,80,128]{2,1,0:T(8,128)(2,1)}, f32[4,1024]{1,0:T(4,128)S(1)}) custom-call(bf16[160,1024]{1,0:T(8,128)(2,1)S(1)} %copy-done.7, bf16[160,1024]{1,0:T(8,128)(2,1)S(1)} %copy-done.6, bf16[160,1024]{1,0:T(8,128)(2,1)} %collective-permute-done.11.m2, ...), custom_call_target="tpu_custom_call" | custom-call | flops 5000000000 | bytes 1048576 | tf_op jit(solution)/shard_map/middle/pallas_call | solution.py:512
  184.5 6.3 %all-to-all-start.4 = ((bf16[16,80,128]{2,1,0:T(8,128)(2,1)}), bf16[16,80,128]{2,1,0:T(8,128)(2,1)S(1)}, u32[]{:S(2)}, u32[]{:S(2)}) async-start(bf16[16,80,128]{2,1,0:T(8,128)(2,1)} %get-tuple-element.99), calls=%async_computation.5 | async-start | bytes 655360 | tf_op jit(solution)/shard_map/all_to_all | solution.py:69
  190.9 3.1 convolution_convert_fusion
  194.0 7.1 %all-to-all-done.4.do_in = bf16[16,80,128]{2,1,0:T(8,128)(2,1)S(1)} async-done(((bf16[16,80,128]{2,1,0:T(8,128)(2,1)}), bf16[16,80,128]{2,1,0:T(8,128)(2,1)S(1)}, u32[]{:S(2)}, u32[]{:S(2)}) %all-to-all-start.4) | async-done | bytes 327712 | tf_op jit(solution)/shard_map/all_to_all | solution.py:69
  205.5 4.4 %all-to-all-start.5 = ((bf16[16,64,512]{2,1,0:T(8,128)(2,1)}), bf16[16,64,512]{2,1,0:T(8,128)(2,1)S(1)}, u32[]{:S(2)}, u32[]{:S(2)}) async-start(bf16[16,64,512]{2,1,0:T(8,128)(2,1)} %get-tuple-element.106), calls=%async_computation.6 | async-start | bytes 2097152 | tf_op jit(solution)/shard_map/all_to_all | solution.py:69
  209.9 27.7 %attend_back.1 = (bf16[16,240,128]{2,1,0:T(8,128)(2,1)}, bf16[1280,192]{1,0:T(8,128)(2,1)}, bf16[1280,192]{1,0:T(8,128)(2,1)}) custom-call(s32[16]{0:T(128)} %compare_select_fusion.3.at, bf16[1280,128]{1,0:T(8,128)(2,1)} %get-tuple-element.74.q.q_a, bf16[1280,128]{1,0:T(8,128)(2,1)} %get-tuple-element.95.q_b, bf16[1280,128]{1,0:T(8,128)(2,1)} %get-tuple-element.75.kv_a, ...), custom_call_target="tpu_custom_call" | custom-call | flops 20000000000 | bytes 1048576 | tf_op jit(solution)/shard_map/attend_back/pallas_call | solution.py:310
  238.6 5.5 %all-to-all-start.6 = ((bf16[16,240,128]{2,1,0:T(8,128)(2,1)}), bf16[16,240,128]{2,1,0:T(8,128)(2,1)S(1)}, u32[]{:S(2)}, u32[]{:S(2)}) async-start(bf16[16,240,128]{2,1,0:T(8,128)(2,1)} %get-tuple-element.107), calls=%async_computation.7 | async-start | bytes 1966080 | tf_op jit(solution)/shard_map/all_to_all | solution.py:69
  244.1 2.7 fusion.13
  247.9 1.6 dynamic-slice_bitcast_fusion.2
  249.5 2.7 collective-permute-start.15
  254.0 2.0 convert_reduce_fusion.1
  256.0 5.4 %all-to-all-done.6.g_a.g_b = bf16[16,240,128]{2,1,0:T(8,128)(2,1)S(1)} async-done(((bf16[16,240,128]{2,1,0:T(8,128)(2,1)}), bf16[16,240,128]{2,1,0:T(8,128)(2,1)S(1)}, u32[]{:S(2)}, u32[]{:S(2)}) %all-to-all-start.6) | async-done | bytes 983072 | tf_op jit(solution)/shard_map/all_to_all | solution.py:69
  261.4 3.4 %all-to-all-start.8 = ((f32[8,8,512]{2,1,0:T(8,128)}), f32[8,8,512]{2,1,0:T(8,128)S(1)}, u32[]{:S(2)}, u32[]{:S(2)}) async-start(f32[8,8,512]{2,1,0:T(8,128)} %bitcast.56), calls=%async_computation.10 | async-start | bytes 262144 | tf_op jit(solution)/shard_map/all_to_all | solution.py:69
  265.8 6.3 %last.1 = (bf16[160,1024]{1,0:T(8,128)(2,1)}, f32[2,1024]{1,0:T(2,128)S(1)}, f32[8,1,384]{2,1,0:T(1,128)S(1)}) custom-call(bf16[16,240,128]{2,1,0:T(8,128)(2,1)S(1)} %all-to-all-done.6.g_a.g_b, bf16[16,240,128]{2,1,0:T(8,128)(2,1)S(1)} %all-to-all-done.6.g_a.g_b, bf16[8,1024,384]{2,1,0:T(8,128)(2,1)} %bitcast.138, bf16[160,1024]{1,0:T(8,128)(2,1)S(1)} %copy-done.3, ...), custom_call_target="tpu_custom_call" | custom-call | flops 15000000512 | bytes 1048576 | tf_op jit(solution)/shard_map/last/pallas_call | solution.py:554
  273.2 1.1 pad_maximum_fusion.1
  274.3 2.5 collective-permute-start.18
  277.1 1.3 collective-permute-start.16
  278.4 9.4 %all-to-all-start.7 = ((bf16[128,8,224]{2,1,0:T(8,128)(2,1)}), bf16[128,8,224]{2,1,0:T(8,128)(2,1)S(1)}, u32[]{:S(2)}, u32[]{:S(2)}) async-start(bf16[128,8,224]{2,1,0:T(8,128)(2,1)} %pad_maximum_fusion.1), calls=%async_computation.9 | async-start | bytes 1048576 | tf_op jit(solution)/shard_map/all_to_all | solution.py:69
  287.8 1.8 add_convert_fusion
  291.7 2.1 convert_reduce_fusion
  293.8 7.1 %all-to-all-done.7 = bf16[128,8,224]{2,1,0:T(8,128)(2,1)S(1)} async-done(((bf16[128,8,224]{2,1,0:T(8,128)(2,1)}), bf16[128,8,224]{2,1,0:T(8,128)(2,1)S(1)}, u32[]{:S(2)}, u32[]{:S(2)}) %all-to-all-start.7) | async-done | bytes 458784 | tf_op jit(solution)/shard_map/all_to_all | solution.py:69
  (182 shorter events, 28.2 us)
Async XLA Ops:
  7.2 19.7 %copy-start.22 = (bf16[8,1024]{1,0:T(8,128)(2,1)S(1)}, bf16[8,1024]{1,0:T(8,128)(2,1)}, u32[]{:S(2)}) copy-start(bf16[8,1024]{1,0:T(8,128)(2,1)} %param.23) | copy-start | bytes 49156
  7.2 54.1 %all-gather.7.cloned.1.call-start = ((), (), s32[]{:S(2)}) async-start(), calls=%async_computation.11 | async-start | bytes 2949120 | tf_op jit(solution)/shard_map/all_gather | solution.py:603
  7.9 59.7 %all-gather.9.cloned.1.call-start = ((), (), s32[]{:S(2)}) async-start(), calls=%async_computation.12 | async-start | bytes 2949120 | tf_op jit(solution)/shard_map/all_gather | solution.py:613
  8.0 18.1 %collective-permute-start = (bf16[160,1024]{1,0:T(8,128)(2,1)}, bf16[160,1024]{1,0:T(8,128)(2,1)S(1)}, u32[]{:S(2)}, u32[]{:S(2)}) collective-permute-start(bf16[160,1024]{1,0:T(8,128)(2,1)} %x.7), channel_id=1, source_target_pairs={{0,8},{8,0},{1,9},{9,1},{2,10},{10,2},{3,11},{11,3},{4,12},{12,4},... | collective-permute-start | bytes 983048 | tf_op jit(solution)/shard_map/ppermute | solution.py:48
  26.8 81.3 %all-gather.11.cloned.1.call-start = ((), (), s32[]{:S(2)}) async-start(), calls=%async_computation.15 | async-start | bytes 5308416 | tf_op jit(solution)/shard_map/all_gather | solution.py:624
  26.8 24.9 %copy-start.2 = (bf16[160,1024]{1,0:T(8,128)(2,1)S(1)}, bf16[160,1024]{1,0:T(8,128)(2,1)}, u32[]{:S(2)}) copy-start(bf16[160,1024]{1,0:T(8,128)(2,1)} %dy.1) | copy-start | bytes 983044
  27.0 25.7 %copy-start.18 = (bf16[32,1024]{1,0:T(8,128)(2,1)S(1)}, bf16[32,1024]{1,0:T(8,128)(2,1)}, u32[]{:S(2)}) copy-start(bf16[32,1024]{1,0:T(8,128)(2,1)} %param.29) | copy-start | bytes 196612
  27.1 25.7 %copy-start.24 = (bf16[32]{0:T(256)(128)(2,1)S(1)}, bf16[32]{0:T(256)(128)(2,1)}, u32[]{:S(2)}) copy-start(bf16[32]{0:T(256)(128)(2,1)} %param.28) | copy-start | bytes 196
  51.7 8.7 %copy-start.10 = (bf16[16,40,1024]{2,1,0:T(8,128)(2,1)}, bf16[16,40,1024]{2,1,0:T(8,128)(2,1)S(1)}, u32[]{:S(2)}) copy-start(bf16[16,40,1024]{2,1,0:T(8,128)(2,1)S(1)} %all_to_all.46.w) | copy-start | bytes 3932164
  54.5 49.9 %all-to-all-start.2 = ((bf16[16,72,1024]{2,1,0:T(8,128)(2,1)}), bf16[16,72,1024]{2,1,0:T(8,128)(2,1)}, u32[]{:S(2)}, u32[]{:S(2)}) async-start(bf16[16,72,1024]{2,1,0:T(8,128)(2,1)} %broadcast_in_dim.75), calls=%async_computation.2 | async-start | bytes 4718592 | tf_op jit(solution)/shard_map/all_to_all | solution.py:69
  59.1 125.4 %all-gather.13.cloned.1.call-start = ((), (), s32[]{:S(2)}) async-start(), calls=%async_computation.16 | async-start | bytes 7077888 | tf_op jit(solution)/shard_map/all_gather | solution.py:641
  88.8 14.1 %collective-permute-start.1 = (bf16[1280,64]{1,0:T(8,128)(2,1)}, bf16[1280,64]{1,0:T(8,128)(2,1)S(1)}, u32[]{:S(2)}, u32[]{:S(2)}) collective-permute-start(bf16[1280,64]{1,0:T(8,128)(2,1)} %get-tuple-element.73), channel_id=1, source_target_pairs={{0,8},{8,0},{1,9},{9,1},{2,10},{10,2},{3,11},{11,3},{4,12},{12,4},... | collective-permute-start | bytes 491528 | tf_op jit(solution)/shard_map/ppermute | solution.py:48
  104.4 7.1 %copy-start.14 = (bf16[1280,128]{1,0:T(8,128)(2,1)}, bf16[1280,128]{1,0:T(8,128)(2,1)S(1)}, u32[]{:S(2)}) copy-start(bf16[1280,128]{1,0:T(8,128)(2,1)S(1)} %maximum_select_fusion) | copy-start | bytes 983044
  104.4 10.7 %collective-permute-start.2 = (bf16[1280,128]{1,0:T(8,128)(2,1)S(1)}, bf16[1280,128]{1,0:T(8,128)(2,1)S(1)}, u32[]{:S(2)}, u32[]{:S(2)}) collective-permute-start(bf16[1280,128]{1,0:T(8,128)(2,1)S(1)} %maximum_select_fusion), channel_id=1, source_target_pairs={{0,6},{2,0},{4,2},{6,4},{1,7},{3,1},{5,3},{7,5},{8,14},{10,8},{12,... | collective-permute-start | bytes 983048 | tf_op jit(solution)/shard_map/ppermute | solution.py:48
  106.0 12.2 %collective-permute-start.3 = (bf16[1280,128]{1,0:T(8,128)(2,1)S(1)}, bf16[1280,128]{1,0:T(8,128)(2,1)S(1)}, u32[]{:S(2)}, u32[]{:S(2)}) collective-permute-start(bf16[1280,128]{1,0:T(8,128)(2,1)S(1)} %maximum_select_fusion), channel_id=1, source_target_pairs={{0,4},{2,6},{4,0},{6,2},{1,5},{3,7},{5,1},{7,3},{8,12},{10,14},{12... | collective-permute-start | bytes 983048 | tf_op jit(solution)/shard_map/ppermute | solution.py:48
  107.0 16.9 %collective-permute-start.4 = (bf16[1280,128]{1,0:T(8,128)(2,1)S(1)}, bf16[1280,128]{1,0:T(8,128)(2,1)S(1)}, u32[]{:S(2)}, u32[]{:S(2)}) collective-permute-start(bf16[1280,128]{1,0:T(8,128)(2,1)S(1)} %maximum_select_fusion), channel_id=1, source_target_pairs={{0,2},{2,4},{4,6},{6,0},{1,3},{3,5},{5,7},{7,1},{8,10},{10,12},{12... | collective-permute-start | bytes 983048 | tf_op jit(solution)/shard_map/ppermute | solution.py:48
  111.4 12.5 %collective-permute-start.5 = (bf16[1280,128]{1,0:T(8,128)(2,1)S(1)}, bf16[1280,128]{1,0:T(8,128)(2,1)S(1)}, u32[]{:S(2)}, u32[]{:S(2)}) collective-permute-start(bf16[1280,128]{1,0:T(8,128)(2,1)S(1)} %maximum_select_fusion), channel_id=1, source_target_pairs={{0,1},{1,0},{2,3},{3,2},{4,5},{5,4},{6,7},{7,6},{8,9},{9,8},{10,11... | collective-permute-start | bytes 983048 | tf_op jit(solution)/shard_map/ppermute | solution.py:48
  115.0 10.5 %copy-start.26 = (bf16[1280,128]{1,0:T(8,128)(2,1)}, bf16[1280,128]{1,0:T(8,128)(2,1)S(1)}, u32[]{:S(2)}) copy-start(bf16[1280,128]{1,0:T(8,128)(2,1)S(1)} %collective-permute-done.2) | copy-start | bytes 983044
  115.0 8.9 %collective-permute-start.6 = (bf16[1280,128]{1,0:T(8,128)(2,1)S(1)}, bf16[1280,128]{1,0:T(8,128)(2,1)S(1)}, u32[]{:S(2)}, u32[]{:S(2)}) collective-permute-start(bf16[1280,128]{1,0:T(8,128)(2,1)S(1)} %collective-permute-done.2), channel_id=1, source_target_pairs={{0,1},{1,0},{2,3},{3,2},{4,5},{5,4},{6,7},{7,6},{8,9},{9,8},{10,11... | collective-permute-start | bytes 983048 | tf_op jit(solution)/shard_map/ppermute | solution.py:48
  118.2 7.4 %copy-start.27 = (bf16[1280,128]{1,0:T(8,128)(2,1)}, bf16[1280,128]{1,0:T(8,128)(2,1)S(1)}, u32[]{:S(2)}) copy-start(bf16[1280,128]{1,0:T(8,128)(2,1)S(1)} %collective-permute-done.3) | copy-start | bytes 983044
  118.2 5.7 %collective-permute-start.7 = (bf16[1280,128]{1,0:T(8,128)(2,1)S(1)}, bf16[1280,128]{1,0:T(8,128)(2,1)S(1)}, u32[]{:S(2)}, u32[]{:S(2)}) collective-permute-start(bf16[1280,128]{1,0:T(8,128)(2,1)S(1)} %collective-permute-done.3), channel_id=1, source_target_pairs={{0,1},{1,0},{2,3},{3,2},{4,5},{5,4},{6,7},{7,6},{8,9},{9,8},{10,11... | collective-permute-start | bytes 983048 | tf_op jit(solution)/shard_map/ppermute | solution.py:48
  123.9 1.6 collective-permute-start.8
  149.2 5.2 %collective-permute-start.9 = (bf16[4,160,1024]{2,1,0:T(8,128)(2,1)}, bf16[4,160,1024]{2,1,0:T(8,128)(2,1)S(1)}, u32[]{:S(2)}, u32[]{:S(2)}) collective-permute-start(bf16[4,160,1024]{2,1,0:T(8,128)(2,1)} %get-tuple-element.87), channel_id=1, source_target_pairs={{0,1},{1,0},{2,3},{3,2},{4,5},{5,4},{6,7},{7,6},{8,9},{9,8},{10,11... | collective-permute-start | bytes 3932168 | tf_op jit(solution)/shard_map/ppermute | solution.py:48
  149.4 24.0 %all-to-all-start.3 = ((bf16[16,32,1024]{2,1,0:T(8,128)(2,1)}), bf16[16,32,1024]{2,1,0:T(8,128)(2,1)}, u32[]{:S(2)}, u32[]{:S(2)}) async-start(bf16[16,32,1024]{2,1,0:T(8,128)(2,1)} %get-tuple-element.89), calls=%async_computation.3 | async-start | bytes 2097152 | tf_op jit(solution)/shard_map/all_to_all | solution.py:69
  155.5 22.9 %copy-start = (bf16[16,8,8,1024]{3,2,1,0:T(8,128)(2,1)S(1)}, bf16[16,8,8,1024]{3,2,1,0:T(8,128)(2,1)}, u32[]{:S(2)}) copy-start(bf16[16,8,8,1024]{3,2,1,0:T(8,128)(2,1)} %copy.107) | copy-start | bytes 6291460
  155.5 22.9 %copy-start.1 = (f32[160,1024]{1,0:T(8,128)S(1)}, f32[160,1024]{1,0:T(8,128)}, u32[]{:S(2)}) copy-start(f32[160,1024]{1,0:T(8,128)} %get-tuple-element.84.resid) | copy-start | bytes 1966084
  155.5 22.9 %copy-start.4 = (bf16[1024,8]{0,1:T(8,128)(2,1)S(1)}, bf16[1024,8]{0,1:T(8,128)(2,1)}, u32[]{:S(2)}) copy-start(bf16[1024,8]{0,1:T(8,128)(2,1)} %copy.120) | copy-start | bytes 49156
  159.5 18.2 %collective-permute-start.10 = (bf16[160,1024]{1,0:T(8,128)(2,1)}, bf16[160,1024]{1,0:T(8,128)(2,1)S(1)}, u32[]{:S(2)}, u32[]{:S(2)}) collective-permute-start(bf16[160,1024]{1,0:T(8,128)(2,1)} %get-tuple-element.91), channel_id=1, source_target_pairs={{0,2},{2,4},{4,6},{6,0},{1,3},{3,5},{5,7},{7,1},{8,10},{10,12},{12... | collective-permute-start | bytes 983048 | tf_op jit(solution)/shard_map/ppermute | solution.py:48
  159.5 18.9 %collective-permute-start.11 = (bf16[160,1024]{1,0:T(8,128)(2,1)}, bf16[160,1024]{1,0:T(8,128)(2,1)}, u32[]{:S(2)}, u32[]{:S(2)}) collective-permute-start(bf16[160,1024]{1,0:T(8,128)(2,1)} %get-tuple-element.92), channel_id=1, source_target_pairs={{0,4},{2,6},{4,0},{6,2},{1,5},{3,7},{5,1},{7,3},{8,12},{10,14},{12... | collective-permute-start | bytes 983048 | tf_op jit(solution)/shard_map/ppermute | solution.py:48
  161.9 16.5 %collective-permute-start.12 = (bf16[160,1024]{1,0:T(8,128)(2,1)}, bf16[160,1024]{1,0:T(8,128)(2,1)}, u32[]{:S(2)}, u32[]{:S(2)}) collective-permute-start(bf16[160,1024]{1,0:T(8,128)(2,1)} %get-tuple-element.93), channel_id=1, source_target_pairs={{0,6},{2,0},{4,2},{6,4},{1,7},{3,1},{5,3},{7,5},{8,14},{10,8},{12,... | collective-permute-start | bytes 983048 | tf_op jit(solution)/shard_map/ppermute | solution.py:48
  184.5 16.6 %all-to-all-start.4 = ((bf16[16,80,128]{2,1,0:T(8,128)(2,1)}), bf16[16,80,128]{2,1,0:T(8,128)(2,1)S(1)}, u32[]{:S(2)}, u32[]{:S(2)}) async-start(bf16[16,80,128]{2,1,0:T(8,128)(2,1)} %get-tuple-element.99), calls=%async_computation.5 | async-start | bytes 655360 | tf_op jit(solution)/shard_map/all_to_all | solution.py:69
  190.8 57.1 %reduce-scatter.5.cloned.1.call-start = ((), (), s32[]{:S(2)}) async-start(), calls=%async_computation.14 | async-start | bytes 2359296 | tf_op jit(solution)/shard_map/reduce_scatter | solution.py:660
  190.9 12.0 %copy-start.23 = (f32[1,512]{1,0:T(1,128)S(1)}, f32[1,512]{1,0:T(1,128)}, u32[]{:S(2)}) copy-start(f32[1,512]{1,0:T(1,128)} %get-tuple-element.122) | copy-start | bytes 6148
  201.1 86.7 %reduce-scatter.3.cloned.1.call-start = ((), (), s32[]{:S(2)}) async-start(), calls=%async_computation.13 | async-start | bytes 2949120 | tf_op jit(solution)/shard_map/reduce_scatter | solution.py:668
  205.5 32.1 %all-to-all-start.5 = ((bf16[16,64,512]{2,1,0:T(8,128)(2,1)}), bf16[16,64,512]{2,1,0:T(8,128)(2,1)S(1)}, u32[]{:S(2)}, u32[]{:S(2)}) async-start(bf16[16,64,512]{2,1,0:T(8,128)(2,1)} %get-tuple-element.106), calls=%async_computation.6 | async-start | bytes 2097152 | tf_op jit(solution)/shard_map/all_to_all | solution.py:69
  238.6 22.8 %all-to-all-start.6 = ((bf16[16,240,128]{2,1,0:T(8,128)(2,1)}), bf16[16,240,128]{2,1,0:T(8,128)(2,1)S(1)}, u32[]{:S(2)}, u32[]{:S(2)}) async-start(bf16[16,240,128]{2,1,0:T(8,128)(2,1)} %get-tuple-element.107), calls=%async_computation.7 | async-start | bytes 1966080 | tf_op jit(solution)/shard_map/all_to_all | solution.py:69
  247.7 18.1 %copy-start.3 = (bf16[160,1024]{1,0:T(8,128)(2,1)S(1)}, bf16[160,1024]{1,0:T(8,128)(2,1)}, u32[]{:S(2)}) copy-start(bf16[160,1024]{1,0:T(8,128)(2,1)} %x.7) | copy-start | bytes 983044
  247.7 18.1 %copy-start.9 = (f32[160,1024]{1,0:T(8,128)S(1)}, f32[160,1024]{1,0:T(8,128)}, u32[]{:S(2)}) copy-start(f32[160,1024]{1,0:T(8,128)} %copy-done.8) | copy-start | bytes 1966084
  249.5 15.3 %collective-permute-start.15 = (bf16[2,2,8,1024]{3,2,1,0:T(8,128)(2,1)}, bf16[2,2,8,1024]{3,2,1,0:T(8,128)(2,1)S(1)}, u32[]{:S(2)}, u32[]{:S(2)}) collective-permute-start(bf16[2,2,8,1024]{3,2,1,0:T(8,128)(2,1)} %get-tuple-element.130), channel_id=1, source_target_pairs={{0,96},{32,0},{64,32},{96,64},{1,97},{33,1},{65,33},{97,65},{2,98}... | collective-permute-start | bytes 196616 | tf_op jit(solution)/shard_map/ppermute | solution.py:48
  252.3 12.5 %collective-permute-start.14 = (bf16[2,2,8,1024]{3,2,1,0:T(8,128)(2,1)}, bf16[2,2,8,1024]{3,2,1,0:T(8,128)(2,1)S(1)}, u32[]{:S(2)}, u32[]{:S(2)}) collective-permute-start(bf16[2,2,8,1024]{3,2,1,0:T(8,128)(2,1)} %get-tuple-element.131), channel_id=1, source_target_pairs={{0,64},{32,96},{64,0},{96,32},{1,65},{33,97},{65,1},{97,33},{2,66}... | collective-permute-start | bytes 196616 | tf_op jit(solution)/shard_map/ppermute | solution.py:48
  253.1 11.7 %collective-permute-start.13 = (bf16[2,2,8,1024]{3,2,1,0:T(8,128)(2,1)S(1)}, bf16[2,2,8,1024]{3,2,1,0:T(8,128)(2,1)}, u32[]{:S(2)}, u32[]{:S(2)}) collective-permute-start(bf16[2,2,8,1024]{3,2,1,0:T(8,128)(2,1)S(1)} %get-tuple-element.129), channel_id=1, source_target_pairs={{0,32},{32,64},{64,96},{96,0},{1,33},{33,65},{65,97},{97,1},{2,34}... | collective-permute-start | bytes 196616 | tf_op jit(solution)/shard_map/ppermute | solution.py:48
  261.4 16.9 %all-to-all-start.8 = ((f32[8,8,512]{2,1,0:T(8,128)}), f32[8,8,512]{2,1,0:T(8,128)S(1)}, u32[]{:S(2)}, u32[]{:S(2)}) async-start(f32[8,8,512]{2,1,0:T(8,128)} %bitcast.56), calls=%async_computation.10 | async-start | bytes 262144 | tf_op jit(solution)/shard_map/all_to_all | solution.py:69
  272.1 15.7 %copy-start.21 = (f32[1,1024]{1,0:T(1,128)S(1)}, f32[1,1024]{1,0:T(1,128)}, u32[]{:S(2)}) copy-start(f32[1,1024]{1,0:T(1,128)} %slice_convert_fusion) | copy-start | bytes 12292
  274.3 16.7 %collective-permute-start.18 = (bf16[8,1024]{1,0:T(8,128)(2,1)S(1)}, bf16[8,1024]{1,0:T(8,128)(2,1)S(1)}, u32[]{:S(2)}, u32[]{:S(2)}) collective-permute-start(bf16[8,1024]{1,0:T(8,128)(2,1)S(1)} %get-tuple-element.137), channel_id=1, source_target_pairs={{0,24},{8,16},{16,0},{24,8},{1,25},{9,17},{17,1},{25,9},{2,26},{10... | collective-permute-start | bytes 49160 | tf_op jit(solution)/shard_map/ppermute | solution.py:57
  276.8 14.2 %collective-permute-start.17 = (bf16[8,1024]{1,0:T(8,128)(2,1)S(1)}, bf16[8,1024]{1,0:T(8,128)(2,1)S(1)}, u32[]{:S(2)}, u32[]{:S(2)}) collective-permute-start(bf16[8,1024]{1,0:T(8,128)(2,1)S(1)} %get-tuple-element.138), channel_id=1, source_target_pairs={{0,8},{8,0},{16,24},{24,16},{1,9},{9,1},{17,25},{25,17},{2,10},{10... | collective-permute-start | bytes 49160 | tf_op jit(solution)/shard_map/ppermute | solution.py:57
  277.1 13.9 %collective-permute-start.16 = (bf16[8,1024]{1,0:T(8,128)(2,1)S(1)}, bf16[8,1024]{1,0:T(8,128)(2,1)S(1)}, u32[]{:S(2)}, u32[]{:S(2)}) collective-permute-start(bf16[8,1024]{1,0:T(8,128)(2,1)S(1)} %get-tuple-element.136), channel_id=1, source_target_pairs={{0,16},{8,24},{16,8},{24,0},{1,17},{9,25},{17,9},{25,1},{2,18},{10... | collective-permute-start | bytes 49160 | tf_op jit(solution)/shard_map/ppermute | solution.py:57
  278.4 22.5 %all-to-all-start.7 = ((bf16[128,8,224]{2,1,0:T(8,128)(2,1)}), bf16[128,8,224]{2,1,0:T(8,128)(2,1)S(1)}, u32[]{:S(2)}, u32[]{:S(2)}) async-start(bf16[128,8,224]{2,1,0:T(8,128)(2,1)} %pad_maximum_fusion.1), calls=%async_computation.9 | async-start | bytes 1048576 | tf_op jit(solution)/shard_map/all_to_all | solution.py:69
  291.0 2.8 collective-permute-start.19
  (18 other events, 42.5 us)
Sparse Core Ops, SparseCore 0:
  9.7 28.8 all-gather.6
  40.9 26.6 all-gather.8
  69.3 34.9 all-gather.10
  125.7 38.3 all-gather.12
  201.2 31.3 reduce-scatter.4
  234.8 41.1 reduce-scatter.2
where the time goes:
time: 314 us; the launch traced here: 311 us
  Pallas kernels  96.3 us (31%)
  starting transfers between devices  62.2 us (20%)
  waiting for transfers between devices  55.3 us (18%)
  blocking collectives  35.9 us (11%)
  local copies, waits for them, and re-layouts  26.1 us (8%)
  between operations  15.2 us (5%)
  other arithmetic  13.6 us (4%)
  matrix products  6.58 us (2%)
    all_to_all x7, starting transfers between devices, exchange(): return lax.all_to_all(value, axes, split_axis=0, concat_axis=0, tiled=True)  38.6 us
    all_to_all x2, blocking collectives, exchange(): return lax.all_to_all(value, axes, split_axis=0, concat_axis=0, tiled=True)  35.9 us
    all_to_all x7, waiting for transfers between devices, exchange(): return lax.all_to_all(value, axes, split_axis=0, concat_axis=0, tiled=True)  29.9 us
    pallas_call x1, Pallas kernels, attend_back(): pl.pallas_call(attend_back_kernel, out_shape=(jax.ShapeDtypeStruct((HEADS...  27.7 us
    pallas_call x1, Pallas kernels, feed(): pl.pallas_call(feed_kernel, out_shape=(jax.ShapeDtypeStruct((TOK, D), F32...  22.9 us
    pallas_call x1, Pallas kernels, project(): pl.pallas_call(project_kernel, out_shape=[tokens] * 2 + [pairs] * 4 + [ja...  21.2 us
    ppermute x16, starting transfers between devices, along(): lax.ppermute(value, axis, [(i, (i + by) % size) for i in range(size)])  18.4 us
    ppermute x16, waiting for transfers between devices, along(): lax.ppermute(value, axis, [(i, (i + by) % size) for i in range(size)])  18.3 us
  transfers between devices with their start and end apart: 33, of which 10 were waited for; matrix products, arithmetic and copies ran while one was open for 11% of the time, Pallas kernels for 31%

commit v1 on v0

--- a/solution.py
+++ b/solution.py
@@ -388,7 +388,9 @@
     y_out[:, 0] = dot(hidden, w2[...]).astype(BF).reshape(4, TOK, D)
     w2_grad[...] += dot(hidden, dy_rows, ((0,), (0,)))
     w1_grad[...] += dot(normed, pre_grad, ((0,), (0,)))
-    b1_out[...] += jnp.sum(pre_grad.astype(F32), 0, keepdims=True)
+    sums = jnp.sum(pre_grad.astype(F32), 0, keepdims=True)
+    for j in range(16):
+        b1_out[j : j + 1, 0:32] += sums[:, j * 32 : j * 32 + 32]
 
     @pl.when(own)
     def _():
@@ -417,7 +419,7 @@
             jax.ShapeDtypeStruct((4, TOK, D), BF),
             jax.ShapeDtypeStruct((16, 64, 512), BF),
             jax.ShapeDtypeStruct((16, 32, D), BF),
-            jax.ShapeDtypeStruct((1, 512), F32),
+            jax.ShapeDtypeStruct((16, 32), F32),
         ),
         grid_spec=pltpu.PrefetchScalarGridSpec(
             num_scalar_prefetch=1,
@@ -439,7 +441,7 @@
                 whole(4, TOK, D),
                 whole(16, 64, 512),
                 whole(16, 32, D),
-                whole(1, 512),
+                whole(16, 32),
             ],
             scratch_shapes=[
                 pltpu.VMEM((4 * TOK, D), BF),
@@ -520,7 +522,7 @@
         grid=(1,),
         in_specs=[whole(TOK, D)] * 6 + [whole(8, D), whole(D, D)],
         out_specs=[whole(TOK, D), whole(TOK, D), whole(HEADS, TOK // 2, 128), whole(4, D)],
-        compiler_params=params(16),
+        compiler_params=params(60),
         cost_estimate=cost(5),
         name="middle",
     )(*parts, resid, dy, sv, w_out)
@@ -683,7 +685,7 @@
     vectors = jnp.concatenate([norm_sums, biases[0:1], biases[2:3], mid_sums])
     vectors = vectors.reshape(8, 128, 8).transpose(1, 0, 2)
     mine = jnp.arange(8)[None, :, None] == zc
-    b1_part = jnp.where(mine, b1_grad.reshape(16, 1, 32), 0.0).reshape(128, 4, 8)
+    b1_part = jnp.where(mine, b1_grad[:, None], 0.0).reshape(128, 4, 8)
     b1_part = jnp.pad(b1_part, ((0, 0), (0, 4), (0, 0)))
     vectors = jnp.concatenate([vectors, b1_part], 2)
     high = vectors.astype(BF)

time: 314 us -> 311 us (level)
  local copies, waits for them, and re-layouts: 26.1 us -> 22.9 us
    unnamed x68 -> x62, local copies, waits for them, and re-layouts: 7.89 us -> 5.12 us
  transfers between devices with their start and end apart: 33 -> 33, of which waited for: 10 -> 11; matrix products, arithmetic and copies ran while one was open for 11% -> 11% of each run, Pallas kernels for 31% -> 32%
where the time goes in v1:
time: 311 us; the launch traced here: 308 us
  Pallas kernels  97.3 us (31%)
  starting transfers between devices  62 us (20%)
  waiting for transfers between devices  56.1 us (18%)
  blocking collectives  35.9 us (12%)
  local copies, waits for them, and re-layouts  22.9 us (7%)
  between operations  15.2 us (5%)
  other arithmetic  11.5 us (4%)
  matrix products  6.81 us (2%)
    all_to_all x7, starting transfers between devices, exchange(): return lax.all_to_all(value, axes, split_axis=0, concat_axis=0, tiled=True)  38.6 us
    all_to_all x2, blocking collectives, exchange(): return lax.all_to_all(value, axes, split_axis=0, concat_axis=0, tiled=True)  35.9 us
    all_to_all x7, waiting for transfers between devices, exchange(): return lax.all_to_all(value, axes, split_axis=0, concat_axis=0, tiled=True)  30.3 us
    pallas_call x1, Pallas kernels, attend_back(): pl.pallas_call(attend_back_kernel, out_shape=(jax.ShapeDtypeStruct((HEADS...  27.6 us
    pallas_call x1, Pallas kernels, feed(): pl.pallas_call(feed_kernel, out_shape=(jax.ShapeDtypeStruct((TOK, D), F32...  22.9 us
    pallas_call x1, Pallas kernels, project(): pl.pallas_call(project_kernel, out_shape=[tokens] * 2 + [pairs] * 4 + [ja...  21.2 us
    ppermute x16, waiting for transfers between devices, along(): lax.ppermute(value, axis, [(i, (i + by) % size) for i in range(size)])  18.8 us
    ppermute x16, starting transfers between devices, along(): lax.ppermute(value, axis, [(i, (i + by) % size) for i in range(size)])  18.4 us
  transfers between devices with their start and end apart: 33, of which 11 were waited for; matrix products, arithmetic and copies ran while one was open for 11% of the time, Pallas kernels for 32%

profile of v1, /device:TPU:0, one launch (start us, length us, event | category | flops | bytes accessed | tf_op | source)
XLA Modules:
  0.0 307.8 jit_solution(12271740016799925100)
XLA Ops:
  8.0 3.4 %collective-permute-start = (bf16[160,1024]{1,0:T(8,128)(2,1)}, bf16[160,1024]{1,0:T(8,128)(2,1)S(1)}, u32[]{:S(2)}, u32[]{:S(2)}) collective-permute-start(bf16[160,1024]{1,0:T(8,128)(2,1)} %x.7), channel_id=1, source_target_pairs={{0,8},{8,0},{1,9},{9,1},{2,10},{10,2},{3,11},{11,3},{4,12},{12,4},... | collective-permute-start | bytes 983048 | tf_op jit(solution)/shard_map/ppermute | solution.py:48
  11.3 1.1 reshape.175
  14.8 11.3 %all_to_all.45 = bf16[8,8,1024]{2,1,0:T(8,128)(2,1)S(1)} all-to-all(bf16[8,8,1024]{2,1,0:T(8,128)(2,1)S(1)} %pad_maximum_fusion.3), channel_id=1, replica_groups=mesh['x'=4,'yl'=2,'yh'=2,'z'=4,'c'=2] {'z','c'}, dimensions={0} | all-to-all | bytes 262144 | tf_op jit(solution)/shard_map/all_to_all | solution.py:69
  27.1 24.7 %all_to_all.46.w = bf16[16,40,1024]{2,1,0:T(8,128)(2,1)S(1)} all-to-all(bf16[16,40,1024]{2,1,0:T(8,128)(2,1)S(1)} %broadcast_in_dim.72), channel_id=1, replica_groups=mesh['x'=4,'yl'=2,'yh'=2,'z'=4,'c'=2] {'x','yl','yh'}, dimensions={0} | all-to-all | bytes 2621440 | tf_op jit(solution)/shard_map/all_to_all | solution.py:69
  52.8 1.7 broadcast_in_dim.74
  54.5 4.6 %all-to-all-start.2 = ((bf16[16,72,1024]{2,1,0:T(8,128)(2,1)}), bf16[16,72,1024]{2,1,0:T(8,128)(2,1)}, u32[]{:S(2)}, u32[]{:S(2)}) async-start(bf16[16,72,1024]{2,1,0:T(8,128)(2,1)} %broadcast_in_dim.74), calls=%async_computation.2 | async-start | bytes 4718592 | tf_op jit(solution)/shard_map/all_to_all | solution.py:69
  61.3 6.3 %all-gather.9.cloned.1.call-done = bf16[1280,1024]{1,0:T(8,128)(2,1)} async-done(((bf16[160,1024]{1,0:T(8,128)(2,1)}), bf16[1280,1024]{1,0:T(8,128)(2,1)}) %all-gather.9.cloned.1.call-update) | async-done | bytes 2621456 | tf_op jit(solution)/shard_map/all_gather | solution.py:615
  67.6 21.2 %project_attend.1 = (bf16[4,2,160,1024]{3,2,1,0:T(8,128)(2,1)}, bf16[4,2,160,1024]{3,2,1,0:T(8,128)(2,1)}, bf16[1280,128]{1,0:T(8,128)(2,1)}, bf16[1280,128]{1,0...) custom-call(s32[16]{0:T(128)} %compare_select_fusion.3.at, ...), custom_call_target="tpu_custom_call" | custom-call | flops 1000000000 | bytes 1048576 | tf_op jit(solution)/shard_map/project_attend/pallas_call | solution.py:174
  88.8 3.1 %collective-permute-start.1 = (bf16[1280,64]{1,0:T(8,128)(2,1)}, bf16[1280,64]{1,0:T(8,128)(2,1)S(1)}, u32[]{:S(2)}, u32[]{:S(2)}) collective-permute-start(bf16[1280,64]{1,0:T(8,128)(2,1)} %get-tuple-element.73), channel_id=1, source_target_pairs={{0,8},{8,0},{1,9},{9,1},{2,10},{10,2},{3,11},{11,3},{4,12},{12,4},... | collective-permute-start | bytes 491528 | tf_op jit(solution)/shard_map/ppermute | solution.py:48
  91.9 11.0 %attend.1 = (bf16[1280,64]{1,0:T(8,128)(2,1)}, f32[64,1280]{1,0:T(8,128)}, f32[5,1,256]{2,1,0:T(1,128)}) custom-call(s32[16]{0:T(128)} %compare_select_fusion.3.at, bf16[1280,128]{1,0:T(8,128)(2,1)} %get-tuple-element.74.q.q_a, bf16[1280,128]{1,0:T(8,128)(2,1)} %get-tuple-element.75.kv_a, bf16[1280,128]{1,0:T(8,128)(2,1)} %get-tuple-element.76.kv_b, ...), custom_call_target="tpu_custom_call" | custom-call | flops 1000000000 | bytes 1048576 | tf_op jit(solution)/shard_map/attend/pallas_call | solution.py:222
  102.9 1.5 maximum_select_fusion
  104.4 1.7 collective-permute-start.2
  107.0 1.1 collective-permute-start.4
  108.1 1.8 slice_bitcast_fusion
  109.9 1.6 copy.107
  111.4 3.6 %collective-permute-done.2 = bf16[1280,128]{1,0:T(8,128)(2,1)S(1)} collective-permute-done((bf16[1280,128]{1,0:T(8,128)(2,1)S(1)}, bf16[1280,128]{1,0:T(8,128)(2,1)S(1)}, u32[]{:S(2)}, u32[]{:S(2)}) %collective-permute-start.2) | collective-permute-done | bytes 327712 | tf_op jit(solution)/shard_map/ppermute | solution.py:48
  115.0 3.2 %collective-permute-done.3 = bf16[1280,128]{1,0:T(8,128)(2,1)S(1)} collective-permute-done((bf16[1280,128]{1,0:T(8,128)(2,1)S(1)}, bf16[1280,128]{1,0:T(8,128)(2,1)S(1)}, u32[]{:S(2)}, u32[]{:S(2)}) %collective-permute-start.3) | collective-permute-done | bytes 327712 | tf_op jit(solution)/shard_map/ppermute | solution.py:48
  118.2 5.7 %collective-permute-done.4 = bf16[1280,128]{1,0:T(8,128)(2,1)S(1)} collective-permute-done((bf16[1280,128]{1,0:T(8,128)(2,1)S(1)}, bf16[1280,128]{1,0:T(8,128)(2,1)S(1)}, u32[]{:S(2)}, u32[]{:S(2)}) %collective-permute-start.4) | collective-permute-done | bytes 327712 | tf_op jit(solution)/shard_map/ppermute | solution.py:48
  124.0 1.6 collective-permute-done.8
  126.3 22.9 %out_feed.1 = (f32[160,1024]{1,0:T(8,128)}, bf16[160,1024]{1,0:T(8,128)(2,1)}, bf16[4,2,160,1024]{3,2,1,0:T(8,128)(2,1)}, bf16[4,160,1024]{2,1,0:T(8,128)(2,1)},...) custom-call(s32[16]{0:T(128)} %compare_select_fusion.3.at, ...), custom_call_target="tpu_custom_call" | custom-call | flops 20000000000 | bytes 1048576 | tf_op jit(solution)/shard_map/out_feed/pallas_call | solution.py:412
  149.4 4.9 %all-to-all-start.3 = ((bf16[16,32,1024]{2,1,0:T(8,128)(2,1)}), bf16[16,32,1024]{2,1,0:T(8,128)(2,1)S(1)}, u32[]{:S(2)}, u32[]{:S(2)}) async-start(bf16[16,32,1024]{2,1,0:T(8,128)(2,1)} %get-tuple-element.89), calls=%async_computation.3 | async-start | bytes 2097152 | tf_op jit(solution)/shard_map/all_to_all | solution.py:69
  154.3 1.1 copy-done.19
  155.5 3.8 %mix.1 = (bf16[160,1024]{1,0:T(8,128)(2,1)}, bf16[160,1024]{1,0:T(8,128)(2,1)}, bf16[160,1024]{1,0:T(8,128)(2,1)}, bf16[160,1024]{1,0:T(8,128)(2,1)}) custom-call(s32[16]{0:T(128)} %compare_select_fusion.3.at, bf16[4,160,1024]{2,1,0:T(8,128)(2,1)} %get-tuple-element.86.own, bf16[4,160,1024]{2,1,0:T(8,128)(2,1)} %copy-done.19), custom_call_target="tpu_custom_call" | custom-call | flops 2000000000 | bytes 1048576 | tf_op jit(solution)/shard_map/mix/pallas_call | solution.py:468
  159.2 2.4 collective-permute-start.11
  161.7 1.2 collective-permute-start.12
  162.8 10.5 %all-to-all-done.3 = bf16[16,32,1024]{2,1,0:T(8,128)(2,1)S(1)} async-done(((bf16[16,32,1024]{2,1,0:T(8,128)(2,1)}), bf16[16,32,1024]{2,1,0:T(8,128)(2,1)S(1)}, u32[]{:S(2)}, u32[]{:S(2)}) %all-to-all-start.3) | async-done | bytes 1048608 | tf_op jit(solution)/shard_map/all_to_all | solution.py:69
  173.3 4.1 %collective-permute-done.10.m1 = bf16[160,1024]{1,0:T(8,128)(2,1)S(1)} collective-permute-done((bf16[160,1024]{1,0:T(8,128)(2,1)}, bf16[160,1024]{1,0:T(8,128)(2,1)S(1)}, u32[]{:S(2)}, u32[]{:S(2)}) %collective-permute-start.10) | collective-permute-done | bytes 327712 | tf_op jit(solution)/shard_map/ppermute | solution.py:48
  178.8 4.5 %middle.1 = (f32[160,1024]{1,0:T(8,128)}, bf16[160,1024]{1,0:T(8,128)(2,1)}, bf16[16,80,128]{2,1,0:T(8,128)(2,1)}, f32[4,1024]{1,0:T(4,128)}) custom-call(bf16[160,1024]{1,0:T(8,128)(2,1)} %get-tuple-element.90.m0, bf16[160,1024]{1,0:T(8,128)(2,1)} %copy-done.27, bf16[160,1024]{1,0:T(8,128)(2,1)} %copy-done.28, bf16[160,1024]{1,0:T(8,128)(2,1)} %copy-done.29, ...), custom_call_target="tpu_custom_call" | custom-call | flops 5000000000 | bytes 1048576 | tf_op jit(solution)/shard_map/middle/pallas_call | solution.py:514
  183.3 6.4 %all-to-all-start.4 = ((bf16[16,80,128]{2,1,0:T(8,128)(2,1)}), bf16[16,80,128]{2,1,0:T(8,128)(2,1)S(1)}, u32[]{:S(2)}, u32[]{:S(2)}) async-start(bf16[16,80,128]{2,1,0:T(8,128)(2,1)} %get-tuple-element.99), calls=%async_computation.5 | async-start | bytes 655360 | tf_op jit(solution)/shard_map/all_to_all | solution.py:69
  189.8 3.1 %convolution_convert_fusion = bf16[1024,1024]{1,0:T(8,128)(2,1)} fusion(bf16[160,1024]{1,0:T(8,128)(2,1)S(1)} %copy-done.12, bf16[160,1024]{1,0:T(8,128)(2,1)} %get-tuple-element.109), kind=kOutput, calls=%fused_computation.3 | convolution fusion | flops 336592896 | bytes 2752512 | tf_op jit(solution)/shard_map/dot_general | solution.py:31
  192.9 7.0 %all-to-all-done.4.do_in = bf16[16,80,128]{2,1,0:T(8,128)(2,1)S(1)} async-done(((bf16[16,80,128]{2,1,0:T(8,128)(2,1)}), bf16[16,80,128]{2,1,0:T(8,128)(2,1)S(1)}, u32[]{:S(2)}, u32[]{:S(2)}) %all-to-all-start.4) | async-done | bytes 327712 | tf_op jit(solution)/shard_map/all_to_all | solution.py:69
  201.1 4.4 %all-to-all-start.5 = ((bf16[16,64,512]{2,1,0:T(8,128)(2,1)}), bf16[16,64,512]{2,1,0:T(8,128)(2,1)S(1)}, u32[]{:S(2)}, u32[]{:S(2)}) async-start(bf16[16,64,512]{2,1,0:T(8,128)(2,1)} %get-tuple-element.106), calls=%async_computation.6 | async-start | bytes 2097152 | tf_op jit(solution)/shard_map/all_to_all | solution.py:69
  205.5 27.6 %attend_back.1 = (bf16[16,240,128]{2,1,0:T(8,128)(2,1)}, bf16[1280,192]{1,0:T(8,128)(2,1)}, bf16[1280,192]{1,0:T(8,128)(2,1)}) custom-call(s32[16]{0:T(128)} %compare_select_fusion.3.at, bf16[1280,128]{1,0:T(8,128)(2,1)} %get-tuple-element.74.q.q_a, bf16[1280,128]{1,0:T(8,128)(2,1)} %get-tuple-element.95.q_b, bf16[1280,128]{1,0:T(8,128)(2,1)} %get-tuple-element.75.kv_a, ...), custom_call_target="tpu_custom_call" | custom-call | flops 20000000000 | bytes 1048576 | tf_op jit(solution)/shard_map/attend_back/pallas_call | solution.py:310
  234.1 5.6 %all-to-all-start.6 = ((bf16[16,240,128]{2,1,0:T(8,128)(2,1)}), bf16[16,240,128]{2,1,0:T(8,128)(2,1)S(1)}, u32[]{:S(2)}, u32[]{:S(2)}) async-start(bf16[16,240,128]{2,1,0:T(8,128)(2,1)} %get-tuple-element.107), calls=%async_computation.7 | async-start | bytes 1966080 | tf_op jit(solution)/shard_map/all_to_all | solution.py:69
  239.8 3.0 fusion.13
  243.6 1.0 copy.108
  244.7 1.6 dynamic-slice_bitcast_fusion.2
  246.2 2.7 collective-permute-start.15
  250.7 2.0 convert_reduce_fusion.1
  252.7 4.4 %all-to-all-done.6.g_a.g_b = bf16[16,240,128]{2,1,0:T(8,128)(2,1)S(1)} async-done(((bf16[16,240,128]{2,1,0:T(8,128)(2,1)}), bf16[16,240,128]{2,1,0:T(8,128)(2,1)S(1)}, u32[]{:S(2)}, u32[]{:S(2)}) %all-to-all-start.6) | async-done | bytes 983072 | tf_op jit(solution)/shard_map/all_to_all | solution.py:69
  257.1 3.4 %all-to-all-start.8 = ((f32[8,8,512]{2,1,0:T(8,128)}), f32[8,8,512]{2,1,0:T(8,128)S(1)}, u32[]{:S(2)}, u32[]{:S(2)}) async-start(f32[8,8,512]{2,1,0:T(8,128)} %bitcast.56), calls=%async_computation.10 | async-start | bytes 262144 | tf_op jit(solution)/shard_map/all_to_all | solution.py:69
  261.4 6.4 %last.1 = (bf16[160,1024]{1,0:T(8,128)(2,1)}, f32[2,1024]{1,0:T(2,128)S(1)}, f32[8,1,384]{2,1,0:T(1,128)S(1)}) custom-call(bf16[16,240,128]{2,1,0:T(8,128)(2,1)S(1)} %all-to-all-done.6.g_a.g_b, bf16[16,240,128]{2,1,0:T(8,128)(2,1)S(1)} %all-to-all-done.6.g_a.g_b, bf16[8,1024,384]{2,1,0:T(8,128)(2,1)} %bitcast.138, bf16[160,1024]{1,0:T(8,128)(2,1)S(1)} %copy-done, ...), custom_call_target="tpu_custom_call" | custom-call | flops 15000000512 | bytes 1048576 | tf_op jit(solution)/shard_map/last/pallas_call | solution.py:556
  268.9 2.1 pad_maximum_fusion.1
  271.0 2.5 collective-permute-start.18
  273.8 1.3 collective-permute-start.16
  275.1 9.3 %all-to-all-start.7 = ((bf16[128,8,224]{2,1,0:T(8,128)(2,1)}), bf16[128,8,224]{2,1,0:T(8,128)(2,1)S(1)}, u32[]{:S(2)}, u32[]{:S(2)}) async-start(bf16[128,8,224]{2,1,0:T(8,128)(2,1)} %pad_maximum_fusion.1), calls=%async_computation.9 | async-start | bytes 1048576 | tf_op jit(solution)/shard_map/all_to_all | solution.py:69
  284.5 1.8 add_convert_fusion
  289.2 8.3 %all-to-all-done.7 = bf16[128,8,224]{2,1,0:T(8,128)(2,1)S(1)} async-done(((bf16[128,8,224]{2,1,0:T(8,128)(2,1)}), bf16[128,8,224]{2,1,0:T(8,128)(2,1)S(1)}, u32[]{:S(2)}, u32[]{:S(2)}) %all-to-all-start.7) | async-done | bytes 458784 | tf_op jit(solution)/shard_map/all_to_all | solution.py:69
  (173 shorter events, 23.4 us)
Async XLA Ops:
  7.2 19.7 %copy-start.15 = (bf16[8,1024]{1,0:T(8,128)(2,1)S(1)}, bf16[8,1024]{1,0:T(8,128)(2,1)}, u32[]{:S(2)}) copy-start(bf16[8,1024]{1,0:T(8,128)(2,1)} %param.23) | copy-start | bytes 49156
  7.2 54.1 %all-gather.7.cloned.1.call-start = ((), (), s32[]{:S(2)}) async-start(), calls=%async_computation.11 | async-start | bytes 2949120 | tf_op jit(solution)/shard_map/all_gather | solution.py:605
  7.9 59.7 %all-gather.9.cloned.1.call-start = ((), (), s32[]{:S(2)}) async-start(), calls=%async_computation.12 | async-start | bytes 2949120 | tf_op jit(solution)/shard_map/all_gather | solution.py:615
  8.0 18.1 %collective-permute-start = (bf16[160,1024]{1,0:T(8,128)(2,1)}, bf16[160,1024]{1,0:T(8,128)(2,1)S(1)}, u32[]{:S(2)}, u32[]{:S(2)}) collective-permute-start(bf16[160,1024]{1,0:T(8,128)(2,1)} %x.7), channel_id=1, source_target_pairs={{0,8},{8,0},{1,9},{9,1},{2,10},{10,2},{3,11},{11,3},{4,12},{12,4},... | collective-permute-start | bytes 983048 | tf_op jit(solution)/shard_map/ppermute | solution.py:48
  26.8 81.3 %all-gather.11.cloned.1.call-start = ((), (), s32[]{:S(2)}) async-start(), calls=%async_computation.15 | async-start | bytes 5308416 | tf_op jit(solution)/shard_map/all_gather | solution.py:626
  26.8 24.9 %copy-start.8 = (bf16[160,1024]{1,0:T(8,128)(2,1)S(1)}, bf16[160,1024]{1,0:T(8,128)(2,1)}, u32[]{:S(2)}) copy-start(bf16[160,1024]{1,0:T(8,128)(2,1)} %dy.1) | copy-start | bytes 983044
  27.0 25.7 %copy-start.13 = (bf16[32,1024]{1,0:T(8,128)(2,1)S(1)}, bf16[32,1024]{1,0:T(8,128)(2,1)}, u32[]{:S(2)}) copy-start(bf16[32,1024]{1,0:T(8,128)(2,1)} %param.29) | copy-start | bytes 196612
  27.1 25.7 %copy-start.18 = (bf16[32]{0:T(256)(128)(2,1)S(1)}, bf16[32]{0:T(256)(128)(2,1)}, u32[]{:S(2)}) copy-start(bf16[32]{0:T(256)(128)(2,1)} %param.28) | copy-start | bytes 196
  51.7 8.7 %copy-start.3 = (bf16[16,40,1024]{2,1,0:T(8,128)(2,1)}, bf16[16,40,1024]{2,1,0:T(8,128)(2,1)S(1)}, u32[]{:S(2)}) copy-start(bf16[16,40,1024]{2,1,0:T(8,128)(2,1)S(1)} %all_to_all.46.w) | copy-start | bytes 3932164
  54.5 49.9 %all-to-all-start.2 = ((bf16[16,72,1024]{2,1,0:T(8,128)(2,1)}), bf16[16,72,1024]{2,1,0:T(8,128)(2,1)}, u32[]{:S(2)}, u32[]{:S(2)}) async-start(bf16[16,72,1024]{2,1,0:T(8,128)(2,1)} %broadcast_in_dim.74), calls=%async_computation.2 | async-start | bytes 4718592 | tf_op jit(solution)/shard_map/all_to_all | solution.py:69
  59.1 124.2 %all-gather.13.cloned.1.call-start = ((), (), s32[]{:S(2)}) async-start(), calls=%async_computation.16 | async-start | bytes 7077888 | tf_op jit(solution)/shard_map/all_gather | solution.py:643
  88.8 14.1 %collective-permute-start.1 = (bf16[1280,64]{1,0:T(8,128)(2,1)}, bf16[1280,64]{1,0:T(8,128)(2,1)S(1)}, u32[]{:S(2)}, u32[]{:S(2)}) collective-permute-start(bf16[1280,64]{1,0:T(8,128)(2,1)} %get-tuple-element.73), channel_id=1, source_target_pairs={{0,8},{8,0},{1,9},{9,1},{2,10},{10,2},{3,11},{11,3},{4,12},{12,4},... | collective-permute-start | bytes 491528 | tf_op jit(solution)/shard_map/ppermute | solution.py:48
  104.4 7.1 %copy-start.9 = (bf16[1280,128]{1,0:T(8,128)(2,1)}, bf16[1280,128]{1,0:T(8,128)(2,1)S(1)}, u32[]{:S(2)}) copy-start(bf16[1280,128]{1,0:T(8,128)(2,1)S(1)} %maximum_select_fusion) | copy-start | bytes 983044
  104.4 10.7 %collective-permute-start.2 = (bf16[1280,128]{1,0:T(8,128)(2,1)S(1)}, bf16[1280,128]{1,0:T(8,128)(2,1)S(1)}, u32[]{:S(2)}, u32[]{:S(2)}) collective-permute-start(bf16[1280,128]{1,0:T(8,128)(2,1)S(1)} %maximum_select_fusion), channel_id=1, source_target_pairs={{0,6},{2,0},{4,2},{6,4},{1,7},{3,1},{5,3},{7,5},{8,14},{10,8},{12,... | collective-permute-start | bytes 983048 | tf_op jit(solution)/shard_map/ppermute | solution.py:48
  106.0 12.2 %collective-permute-start.3 = (bf16[1280,128]{1,0:T(8,128)(2,1)S(1)}, bf16[1280,128]{1,0:T(8,128)(2,1)S(1)}, u32[]{:S(2)}, u32[]{:S(2)}) collective-permute-start(bf16[1280,128]{1,0:T(8,128)(2,1)S(1)} %maximum_select_fusion), channel_id=1, source_target_pairs={{0,4},{2,6},{4,0},{6,2},{1,5},{3,7},{5,1},{7,3},{8,12},{10,14},{12... | collective-permute-start | bytes 983048 | tf_op jit(solution)/shard_map/ppermute | solution.py:48
  107.0 16.9 %collective-permute-start.4 = (bf16[1280,128]{1,0:T(8,128)(2,1)S(1)}, bf16[1280,128]{1,0:T(8,128)(2,1)S(1)}, u32[]{:S(2)}, u32[]{:S(2)}) collective-permute-start(bf16[1280,128]{1,0:T(8,128)(2,1)S(1)} %maximum_select_fusion), channel_id=1, source_target_pairs={{0,2},{2,4},{4,6},{6,0},{1,3},{3,5},{5,7},{7,1},{8,10},{10,12},{12... | collective-permute-start | bytes 983048 | tf_op jit(solution)/shard_map/ppermute | solution.py:48
  111.4 12.5 %collective-permute-start.5 = (bf16[1280,128]{1,0:T(8,128)(2,1)S(1)}, bf16[1280,128]{1,0:T(8,128)(2,1)S(1)}, u32[]{:S(2)}, u32[]{:S(2)}) collective-permute-start(bf16[1280,128]{1,0:T(8,128)(2,1)S(1)} %maximum_select_fusion), channel_id=1, source_target_pairs={{0,1},{1,0},{2,3},{3,2},{4,5},{5,4},{6,7},{7,6},{8,9},{9,8},{10,11... | collective-permute-start | bytes 983048 | tf_op jit(solution)/shard_map/ppermute | solution.py:48
  115.0 10.5 %copy-start.20 = (bf16[1280,128]{1,0:T(8,128)(2,1)}, bf16[1280,128]{1,0:T(8,128)(2,1)S(1)}, u32[]{:S(2)}) copy-start(bf16[1280,128]{1,0:T(8,128)(2,1)S(1)} %collective-permute-done.2) | copy-start | bytes 983044
  115.0 8.9 %collective-permute-start.6 = (bf16[1280,128]{1,0:T(8,128)(2,1)S(1)}, bf16[1280,128]{1,0:T(8,128)(2,1)S(1)}, u32[]{:S(2)}, u32[]{:S(2)}) collective-permute-start(bf16[1280,128]{1,0:T(8,128)(2,1)S(1)} %collective-permute-done.2), channel_id=1, source_target_pairs={{0,1},{1,0},{2,3},{3,2},{4,5},{5,4},{6,7},{7,6},{8,9},{9,8},{10,11... | collective-permute-start | bytes 983048 | tf_op jit(solution)/shard_map/ppermute | solution.py:48
  118.2 7.4 %copy-start.21 = (bf16[1280,128]{1,0:T(8,128)(2,1)}, bf16[1280,128]{1,0:T(8,128)(2,1)S(1)}, u32[]{:S(2)}) copy-start(bf16[1280,128]{1,0:T(8,128)(2,1)S(1)} %collective-permute-done.3) | copy-start | bytes 983044
  118.2 5.7 %collective-permute-start.7 = (bf16[1280,128]{1,0:T(8,128)(2,1)S(1)}, bf16[1280,128]{1,0:T(8,128)(2,1)S(1)}, u32[]{:S(2)}, u32[]{:S(2)}) collective-permute-start(bf16[1280,128]{1,0:T(8,128)(2,1)S(1)} %collective-permute-done.3), channel_id=1, source_target_pairs={{0,1},{1,0},{2,3},{3,2},{4,5},{5,4},{6,7},{7,6},{8,9},{9,8},{10,11... | collective-permute-start | bytes 983048 | tf_op jit(solution)/shard_map/ppermute | solution.py:48
  123.9 1.6 collective-permute-start.8
  149.2 5.1 %collective-permute-start.9 = (bf16[4,160,1024]{2,1,0:T(8,128)(2,1)}, bf16[4,160,1024]{2,1,0:T(8,128)(2,1)S(1)}, u32[]{:S(2)}, u32[]{:S(2)}) collective-permute-start(bf16[4,160,1024]{2,1,0:T(8,128)(2,1)} %get-tuple-element.87), channel_id=1, source_target_pairs={{0,1},{1,0},{2,3},{3,2},{4,5},{5,4},{6,7},{7,6},{8,9},{9,8},{10,11... | collective-permute-start | bytes 3932168 | tf_op jit(solution)/shard_map/ppermute | solution.py:48
  149.4 23.9 %all-to-all-start.3 = ((bf16[16,32,1024]{2,1,0:T(8,128)(2,1)}), bf16[16,32,1024]{2,1,0:T(8,128)(2,1)S(1)}, u32[]{:S(2)}, u32[]{:S(2)}) async-start(bf16[16,32,1024]{2,1,0:T(8,128)(2,1)} %get-tuple-element.89), calls=%async_computation.3 | async-start | bytes 2097152 | tf_op jit(solution)/shard_map/all_to_all | solution.py:69
  159.2 18.2 %collective-permute-start.10 = (bf16[160,1024]{1,0:T(8,128)(2,1)}, bf16[160,1024]{1,0:T(8,128)(2,1)S(1)}, u32[]{:S(2)}, u32[]{:S(2)}) collective-permute-start(bf16[160,1024]{1,0:T(8,128)(2,1)} %get-tuple-element.91), channel_id=1, source_target_pairs={{0,2},{2,4},{4,6},{6,0},{1,3},{3,5},{5,7},{7,1},{8,10},{10,12},{12... | collective-permute-start | bytes 983048 | tf_op jit(solution)/shard_map/ppermute | solution.py:48
  159.2 18.2 %collective-permute-start.11 = (bf16[160,1024]{1,0:T(8,128)(2,1)}, bf16[160,1024]{1,0:T(8,128)(2,1)S(1)}, u32[]{:S(2)}, u32[]{:S(2)}) collective-permute-start(bf16[160,1024]{1,0:T(8,128)(2,1)} %get-tuple-element.92), channel_id=1, source_target_pairs={{0,4},{2,6},{4,0},{6,2},{1,5},{3,7},{5,1},{7,3},{8,12},{10,14},{12... | collective-permute-start | bytes 983048 | tf_op jit(solution)/shard_map/ppermute | solution.py:48
  161.7 16.4 %collective-permute-start.12 = (bf16[160,1024]{1,0:T(8,128)(2,1)}, bf16[160,1024]{1,0:T(8,128)(2,1)S(1)}, u32[]{:S(2)}, u32[]{:S(2)}) collective-permute-start(bf16[160,1024]{1,0:T(8,128)(2,1)} %get-tuple-element.93), channel_id=1, source_target_pairs={{0,6},{2,0},{4,2},{6,4},{1,7},{3,1},{5,3},{7,5},{8,14},{10,8},{12,... | collective-permute-start | bytes 983048 | tf_op jit(solution)/shard_map/ppermute | solution.py:48
  178.8 10.9 %copy-start.12 = (bf16[160,1024]{1,0:T(8,128)(2,1)S(1)}, bf16[160,1024]{1,0:T(8,128)(2,1)}, u32[]{:S(2)}) copy-start(bf16[160,1024]{1,0:T(8,128)(2,1)} %get-tuple-element.108) | copy-start | bytes 983044
  183.3 16.6 %all-to-all-start.4 = ((bf16[16,80,128]{2,1,0:T(8,128)(2,1)}), bf16[16,80,128]{2,1,0:T(8,128)(2,1)S(1)}, u32[]{:S(2)}, u32[]{:S(2)}) async-start(bf16[16,80,128]{2,1,0:T(8,128)(2,1)} %get-tuple-element.99), calls=%async_computation.5 | async-start | bytes 655360 | tf_op jit(solution)/shard_map/all_to_all | solution.py:69
  189.7 55.0 %reduce-scatter.5.cloned.1.call-start = ((), (), s32[]{:S(2)}) async-start(), calls=%async_computation.14 | async-start | bytes 2359296 | tf_op jit(solution)/shard_map/reduce_scatter | solution.py:662
  189.7 10.7 %copy-start.1 = (bf16[1024,8]{0,1:T(8,128)(2,1)S(1)}, bf16[1024,8]{0,1:T(8,128)(2,1)}, u32[]{:S(2)}) copy-start(bf16[1024,8]{0,1:T(8,128)(2,1)} %copy.120) | copy-start | bytes 49156
  189.7 10.7 %copy-start.17 = (f32[16,32]{1,0:T(8,128)S(1)}, f32[16,32]{1,0:T(8,128)}, u32[]{:S(2)}) copy-start(f32[16,32]{1,0:T(8,128)} %get-tuple-element.122) | copy-start | bytes 6148
  189.7 11.0 %copy-start.16 = (f32[4,1024]{1,0:T(4,128)S(1)}, f32[4,1024]{1,0:T(4,128)}, u32[]{:S(2)}) copy-start(f32[4,1024]{1,0:T(4,128)} %get-tuple-element.121) | copy-start | bytes 49156
  199.9 84.5 %reduce-scatter.3.cloned.1.call-start = ((), (), s32[]{:S(2)}) async-start(), calls=%async_computation.13 | async-start | bytes 2949120 | tf_op jit(solution)/shard_map/reduce_scatter | solution.py:670
  201.1 32.1 %all-to-all-start.5 = ((bf16[16,64,512]{2,1,0:T(8,128)(2,1)}), bf16[16,64,512]{2,1,0:T(8,128)(2,1)S(1)}, u32[]{:S(2)}, u32[]{:S(2)}) async-start(bf16[16,64,512]{2,1,0:T(8,128)(2,1)} %get-tuple-element.106), calls=%async_computation.6 | async-start | bytes 2097152 | tf_op jit(solution)/shard_map/all_to_all | solution.py:69
  234.1 23.0 %all-to-all-start.6 = ((bf16[16,240,128]{2,1,0:T(8,128)(2,1)}), bf16[16,240,128]{2,1,0:T(8,128)(2,1)S(1)}, u32[]{:S(2)}, u32[]{:S(2)}) async-start(bf16[16,240,128]{2,1,0:T(8,128)(2,1)} %get-tuple-element.107), calls=%async_computation.7 | async-start | bytes 1966080 | tf_op jit(solution)/shard_map/all_to_all | solution.py:69
  243.6 17.8 %copy-start = (bf16[160,1024]{1,0:T(8,128)(2,1)S(1)}, bf16[160,1024]{1,0:T(8,128)(2,1)}, u32[]{:S(2)}) copy-start(bf16[160,1024]{1,0:T(8,128)(2,1)} %x.7) | copy-start | bytes 983044
  243.6 17.8 %copy-start.2 = (f32[160,1024]{1,0:T(8,128)S(1)}, f32[160,1024]{1,0:T(8,128)}, u32[]{:S(2)}) copy-start(f32[160,1024]{1,0:T(8,128)} %get-tuple-element.117.resid_grad) | copy-start | bytes 1966084
  246.2 14.3 %collective-permute-start.15 = (bf16[2,2,8,1024]{3,2,1,0:T(8,128)(2,1)}, bf16[2,2,8,1024]{3,2,1,0:T(8,128)(2,1)S(1)}, u32[]{:S(2)}, u32[]{:S(2)}) collective-permute-start(bf16[2,2,8,1024]{3,2,1,0:T(8,128)(2,1)} %get-tuple-element.130), channel_id=1, source_target_pairs={{0,96},{32,0},{64,32},{96,64},{1,97},{33,1},{65,33},{97,65},{2,98}... | collective-permute-start | bytes 196616 | tf_op jit(solution)/shard_map/ppermute | solution.py:48
  249.0 11.6 %collective-permute-start.14 = (bf16[2,2,8,1024]{3,2,1,0:T(8,128)(2,1)}, bf16[2,2,8,1024]{3,2,1,0:T(8,128)(2,1)S(1)}, u32[]{:S(2)}, u32[]{:S(2)}) collective-permute-start(bf16[2,2,8,1024]{3,2,1,0:T(8,128)(2,1)} %get-tuple-element.131), channel_id=1, source_target_pairs={{0,64},{32,96},{64,0},{96,32},{1,65},{33,97},{65,1},{97,33},{2,66}... | collective-permute-start | bytes 196616 | tf_op jit(solution)/shard_map/ppermute | solution.py:48
  249.8 10.8 %collective-permute-start.13 = (bf16[2,2,8,1024]{3,2,1,0:T(8,128)(2,1)S(1)}, bf16[2,2,8,1024]{3,2,1,0:T(8,128)(2,1)S(1)}, u32[]{:S(2)}, u32[]{:S(2)}) collective-permute-start(bf16[2,2,8,1024]{3,2,1,0:T(8,128)(2,1)S(1)} %get-tuple-element.129), channel_id=1, source_target_pairs={{0,32},{32,64},{64,96},{96,0},{1,33},{33,65},{65,97},{97,1},{2,34}... | collective-permute-start | bytes 196616 | tf_op jit(solution)/shard_map/ppermute | solution.py:48
  257.1 18.0 %all-to-all-start.8 = ((f32[8,8,512]{2,1,0:T(8,128)}), f32[8,8,512]{2,1,0:T(8,128)S(1)}, u32[]{:S(2)}, u32[]{:S(2)}) async-start(f32[8,8,512]{2,1,0:T(8,128)} %bitcast.56), calls=%async_computation.10 | async-start | bytes 262144 | tf_op jit(solution)/shard_map/all_to_all | solution.py:69
  267.8 16.7 %copy-start.6 = (f32[160,1024]{1,0:T(8,128)S(1)}, f32[160,1024]{1,0:T(8,128)}, u32[]{:S(2)}) copy-start(f32[160,1024]{1,0:T(8,128)} %get-tuple-element.84.resid) | copy-start | bytes 1966084
  271.0 16.6 %collective-permute-start.18 = (bf16[8,1024]{1,0:T(8,128)(2,1)S(1)}, bf16[8,1024]{1,0:T(8,128)(2,1)S(1)}, u32[]{:S(2)}, u32[]{:S(2)}) collective-permute-start(bf16[8,1024]{1,0:T(8,128)(2,1)S(1)} %get-tuple-element.137), channel_id=1, source_target_pairs={{0,24},{8,16},{16,0},{24,8},{1,25},{9,17},{17,1},{25,9},{2,26},{10... | collective-permute-start | bytes 49160 | tf_op jit(solution)/shard_map/ppermute | solution.py:57
  273.5 14.1 %collective-permute-start.17 = (bf16[8,1024]{1,0:T(8,128)(2,1)S(1)}, bf16[8,1024]{1,0:T(8,128)(2,1)S(1)}, u32[]{:S(2)}, u32[]{:S(2)}) collective-permute-start(bf16[8,1024]{1,0:T(8,128)(2,1)S(1)} %get-tuple-element.138), channel_id=1, source_target_pairs={{0,8},{8,0},{16,24},{24,16},{1,9},{9,1},{17,25},{25,17},{2,10},{10... | collective-permute-start | bytes 49160 | tf_op jit(solution)/shard_map/ppermute | solution.py:57
  273.8 13.8 %collective-permute-start.16 = (bf16[8,1024]{1,0:T(8,128)(2,1)S(1)}, bf16[8,1024]{1,0:T(8,128)(2,1)S(1)}, u32[]{:S(2)}, u32[]{:S(2)}) collective-permute-start(bf16[8,1024]{1,0:T(8,128)(2,1)S(1)} %get-tuple-element.136), channel_id=1, source_target_pairs={{0,16},{8,24},{16,8},{24,0},{1,17},{9,25},{17,9},{25,1},{2,18},{10... | collective-permute-start | bytes 49160 | tf_op jit(solution)/shard_map/ppermute | solution.py:57
  275.1 22.4 %all-to-all-start.7 = ((bf16[128,8,224]{2,1,0:T(8,128)(2,1)}), bf16[128,8,224]{2,1,0:T(8,128)(2,1)S(1)}, u32[]{:S(2)}, u32[]{:S(2)}) async-start(bf16[128,8,224]{2,1,0:T(8,128)(2,1)} %pad_maximum_fusion.1), calls=%async_computation.9 | async-start | bytes 1048576 | tf_op jit(solution)/shard_map/all_to_all | solution.py:69
  287.7 1.5 collective-permute-start.19
  (15 other events, 24.5 us)
Sparse Core Ops, SparseCore 0:
  9.7 28.8 all-gather.6
  40.9 26.6 all-gather.8
  69.3 34.9 all-gather.10
  125.7 38.3 all-gather.12
  200.1 31.2 reduce-scatter.4
  233.6 42.6 reduce-scatter.2
